TPU v7x, 512 devices: a whole 4x8x8 slice. The times are simulated.
512 devices in a mesh: feed: 32 (over z, x), tm: 16 (over y, core).
Axes of the slice: x: 4, y: 8, z: 8, core: 2. Of those that a mesh axis runs over, the one named last changes fastest.
Arguments:
- voltages: bfloat16 [2, 256, 64, 8192], P(None, 'feed', 'tm'), may hold values from -6 to 6
- channel_lag: int32 [8192], replicated, may hold values from 0 to 2
- offsets: int32 [5, 4096], replicated, may hold values from 0 to 1
Outputs:
- dedispersed: float32 [256, 32, 8192], P('feed', 'tm')
All inputs are finite; a program needn't handle non-finite values.
Results may differ from a plain program's by a relative error of at most 0.00063.
Values may be sent and summed in bfloat16 or wider, within the bound.
No kernel may reach another device: no remote copies, remote signals or barrier semaphores. Data moves between devices by JAX's collectives and lax.ppermute only.
A program may use at most 192 MiB of HBM per device.

v0:
```python
import functools
import math

import jax
import jax.numpy as jnp
import ml_dtypes
import numpy as np
from jax import lax
from jax.experimental import pallas as pl
from jax.experimental.pallas import tpu as pltpu
from jax.sharding import Mesh
from jax.sharding import PartitionSpec as P

DS = 2
SECTIONS = 5
GROUP = 2**SECTIONS
LANES = 128
VMEM_LIMIT = 48 * 1024 * 1024


def dft_tables(feeds):
    hi, big, low = np.meshgrid(np.arange(2), np.arange(feeds // 8), np.arange(4), indexing="ij")
    beam = (8 * big + 4 * hi + low).reshape(-1)
    feed = np.arange(feeds)
    angle = (beam[:, None] * feed[None, :] % feeds) * (2.0 * math.pi / feeds)
    cosine = np.cos(angle) / math.sqrt(feeds)
    sine = np.sin(angle) / math.sqrt(feeds)
    real = np.stack([cosine.reshape(feeds, -1, 8), sine.reshape(feeds, -1, 8)], axis=2)
    imag = np.stack([-sine.reshape(feeds, -1, 8), cosine.reshape(feeds, -1, 8)], axis=2)
    table = np.concatenate([real, imag], axis=0).reshape(2 * feeds, 2 * feeds)
    high = table.astype(ml_dtypes.bfloat16)
    rest = (table - high.astype(np.float64)).astype(ml_dtypes.bfloat16)
    return high, rest


def lane_index(shape):
    return lax.broadcasted_iota(jnp.int32, shape, len(shape) - 1)


def roll(x, by):
    return pltpu.roll(x, by % x.shape[-1], x.ndim - 1)


def swap_blocks(rows):
    lane = lane_index(rows[0].shape)
    low_half = lane < 64
    even = lane % 64 < 32
    mid = [None] * 4
    for n in range(2):
        mid[n] = jnp.where(low_half, rows[n], roll(rows[n + 2], 64))
        mid[n + 2] = jnp.where(low_half, roll(rows[n], 64), rows[n + 2])
    out = [None] * 4
    for n in (0, 2):
        out[n] = jnp.where(even, mid[n], roll(mid[n + 1], 32))
        out[n + 1] = jnp.where(even, roll(mid[n], -32), mid[n + 1])
    return out


def pack_kernel(x_ref, out_ref):
    tiles = x_ref.shape[2] // LANES
    for j in range(tiles):
        lanes = pl.ds(j * LANES, LANES)
        rows = [x_ref[n, :, lanes].astype(jnp.float32) for n in range(4)]
        for g, value in enumerate(swap_blocks(rows)):
            out_ref[4 * j + g] = value.astype(jnp.bfloat16)


def beam_kernel(high_ref, rest_ref, x_ref, out_ref):
    sources, several, cf, lanes = x_ref.shape
    x = jnp.concatenate(
        [x_ref[:, k].reshape(sources * cf, lanes) for k in range(several)], axis=1
    )
    beam = jnp.dot(high_ref[...], x, preferred_element_type=jnp.float32)
    beam = beam + jnp.dot(rest_ref[...], x, preferred_element_type=jnp.float32)
    feeds = beam.shape[0] // 2
    half = feeds // 2
    power = beam[:feeds] * beam[:feeds] + beam[feeds:] * beam[feeds:]
    even = lane_index((half, lanes)) % 64 < 32
    for k in range(several):
        first = power[:half, k * lanes : (k + 1) * lanes]
        second = power[half:, k * lanes : (k + 1) * lanes]
        total = jnp.where(even, first + roll(first, -32), second + roll(second, 32))
        out_ref[k] = (total * (1.0 / DS)).astype(jnp.bfloat16)


def mask_kernel(place_ref, lag_ref, off_ref, out_ref):
    place = place_ref[0]
    per_lag = LANES // GROUP
    lag = lag_ref[pl.ds(place // per_lag, 1), :].astype(jnp.float32)
    lag = jnp.broadcast_to(lag, (8, LANES))
    row = lax.broadcasted_iota(jnp.int32, (LANES, LANES), 0)
    lane = lane_index((LANES, LANES))
    channel = lane % GROUP
    source = (place % per_lag) * GROUP + channel
    pick = (row == source).astype(jnp.float32)
    out_ref[0] = jnp.dot(lag, pick, preferred_element_type=jnp.float32)
    half_group = GROUP // 2
    per_off = LANES // half_group
    for s in range(SECTIONS):
        h = 2**s
        values = off_ref[s, pl.ds(place // per_off, 1), :].astype(jnp.float32)
        values = jnp.broadcast_to(values, (8, LANES))
        pair = h * (channel // (2 * h)) + channel % h
        source = (place % per_off) * half_group + pair
        pick = (row == source).astype(jnp.float32)
        out_ref[s + 1] = jnp.dot(values, pick, preferred_element_type=jnp.float32)


def tree_kernel(core_ref, mask_ref, own_ref, other_ref, out_ref):
    blocks = own_ref.shape[0]
    rows = 16
    lane = lane_index((rows, LANES))
    first_time = lane < 64
    channel = lane % GROUP

    def wide(k):
        part = mask_ref[k]
        return jnp.concatenate([part] * (rows // 8), axis=0)

    zero = jnp.zeros((rows, LANES), jnp.float32)

    def back_one(even, odd):
        s_even, s_odd = [], []
        for y in range(blocks):
            before = odd[y - 1] if y else zero
            s_even.append(roll(jnp.where(first_time, even[y], before), 64))
            s_odd.append(roll(jnp.where(first_time, odd[y], even[y]), 64))
        return s_even, s_odd

    def run(is_odd):
        def step(k, _):
            at = pl.ds(pl.multiple_of(k * rows, rows), rows)
            mine = [own_ref[y, at, :].astype(jnp.float32) for y in range(blocks)]
            theirs = [other_ref[y, at, :].astype(jnp.float32) for y in range(blocks)]
            even, odd = (theirs, mine) if is_odd else (mine, theirs)
            lag = wide(0)
            s_even, s_odd = back_one(even, odd)

            def lagged(now, one, two):
                return jnp.where(lag == 0.0, now, jnp.where(lag == 1.0, one, two))

            new_even = [
                lagged(even[y], s_even[y], odd[y - 1] if y else zero) for y in range(blocks)
            ]
            new_odd = [lagged(odd[y], s_odd[y], even[y]) for y in range(blocks)]
            even, odd = new_even, new_odd
            for s in range(SECTIONS):
                h = 2**s
                off = wide(s + 1) > 0.5
                upper = (channel // h) % 2 == 1
                s_even, s_odd = back_one(even, odd)

                def combine(now, one, two):
                    nearer = jnp.where(off, one, now)
                    farther = jnp.where(off, two, one)
                    return jnp.where(upper, roll(now, h) + farther, now + roll(nearer, -h))

                last = s == SECTIONS - 1
                new_even = new_odd = None
                if not (last and is_odd):
                    new_even = [
                        combine(even[y], s_even[y], odd[y - 1] if y else zero)
                        for y in range(blocks)
                    ]
                if not (last and not is_odd):
                    new_odd = [combine(odd[y], s_odd[y], even[y]) for y in range(blocks)]
                even, odd = new_even, new_odd
            final = odd if is_odd else even
            per = rows // 4
            for y in range(blocks):
                value = final[y] * (1.0 / 2**SECTIONS)
                for q in range(per):
                    out_ref[k * per + q, y] = value[4 * q : 4 * q + 4]
            return 0

        lax.fori_loop(0, own_ref.shape[1] // rows, step, 0)

    @pl.when(core_ref[0] == 0)
    def _():
        run(False)

    @pl.when(core_ref[0] != 0)
    def _():
        run(True)


def unpack_kernel(x_ref, out_ref):
    tiles = x_ref.shape[0] // 2
    lane = lane_index((8, LANES))
    row = lax.broadcasted_iota(jnp.int32, (8, LANES), 0)
    low_half = lane < 64
    top = row < 4
    stay = top == (lane % 64 < 32)
    for j in range(tiles):
        v0 = x_ref[2 * j]
        v1 = x_ref[2 * j + 1]
        u = (jnp.where(low_half, v0, roll(v1, 64)), jnp.where(low_half, roll(v0, 64), v1))
        for t in range(2):
            crossed = pltpu.roll(u[t], 4, 0)
            moved = jnp.where(top, roll(crossed, 32), roll(crossed, -32))
            out_ref[t, :, pl.ds(j * LANES, LANES)] = jnp.where(stay, u[t], moved)


def on_device(high, rest, voltages, channel_lag, offsets):
    parts, local, samp, channels = voltages.shape
    feed_count = lax.axis_size("feed")
    y_count = lax.axis_size("y")
    peers = feed_count * y_count
    cf = parts * local
    params = pltpu.CompilerParams(vmem_limit_bytes=VMEM_LIMIT)
    vmem = pl.BlockSpec(memory_space=pltpu.VMEM)
    smem = pl.BlockSpec(memory_space=pltpu.SMEM)

    rows = voltages.reshape(cf, samp, channels).transpose(1, 0, 2)
    steps = 8
    width = channels // steps
    packed = pl.pallas_call(
        pack_kernel,
        grid=(steps,),
        in_specs=[pl.BlockSpec((samp, cf, width), lambda i: (0, 0, i))],
        out_specs=pl.BlockSpec((width // GROUP, cf, LANES), lambda i: (i, 0, 0)),
        out_shape=jax.ShapeDtypeStruct((peers, cf, LANES), jnp.bfloat16),
        compiler_params=params,
        name="pack",
    )(rows)
    turned = lax.all_to_all(packed, ("feed", "y"), split_axis=0, concat_axis=0, tiled=True)

    place = (lax.axis_index("feed") * y_count + lax.axis_index("y")).reshape(1)
    masks = pl.pallas_call(
        mask_kernel,
        in_specs=[smem, vmem, vmem],
        out_specs=vmem,
        out_shape=jax.ShapeDtypeStruct((SECTIONS + 1, 8, LANES), jnp.float32),
        name="masks",
    )(place, channel_lag.reshape(-1, LANES), offsets.reshape(SECTIONS, -1, LANES))

    several = 2
    beams = 2 * feed_count * local // 2
    turned = turned.reshape(feed_count, y_count, cf, LANES)
    whole = lambda i: (0, 0)
    own = pl.pallas_call(
        beam_kernel,
        grid=(y_count // several,),
        in_specs=[
            pl.BlockSpec(high.shape, whole),
            pl.BlockSpec(rest.shape, whole),
            pl.BlockSpec((feed_count, several, cf, LANES), lambda i: (0, i, 0, 0)),
        ],
        out_specs=pl.BlockSpec((several, beams // 2, LANES), lambda i: (i, 0, 0)),
        out_shape=jax.ShapeDtypeStruct((y_count, beams // 2, LANES), jnp.bfloat16),
        compiler_params=params,
        name="beams",
    )(high, rest, turned)
    other = lax.ppermute(own, "core", [(0, 1), (1, 0)])

    core = lax.axis_index("core").reshape(1)
    trials = pl.pallas_call(
        tree_kernel,
        in_specs=[smem, vmem, vmem, vmem],
        out_specs=vmem,
        out_shape=jax.ShapeDtypeStruct((feed_count, y_count, 4, LANES), jnp.float32),
        compiler_params=params,
        name="tree",
    )(core, masks, own, other)
    trials = trials.reshape(peers, 4, LANES)
    back = lax.all_to_all(trials, ("feed", "y"), split_axis=0, concat_axis=0, tiled=True)

    out = pl.pallas_call(
        unpack_kernel,
        grid=(steps,),
        in_specs=[pl.BlockSpec((peers // 2 // steps, 8, LANES), lambda i: (i, 0, 0))],
        out_specs=pl.BlockSpec((2, 8, width), lambda i: (0, 0, i)),
        out_shape=jax.ShapeDtypeStruct((2, 8, channels), jnp.float32),
        compiler_params=params,
        name="unpack",
    )(back.reshape(peers // 2, 8, LANES))
    return out.transpose(1, 0, 2)


def solution(mesh):
    devices = mesh.devices
    fine = Mesh(devices.reshape(devices.shape[0], -1, 2), ("feed", "y", "core"))
    high, rest = dft_tables(8 * devices.shape[0])
    times = ("y", "core")
    body = jax.shard_map(
        functools.partial(on_device),
        mesh=fine,
        in_specs=(P(), P(), P(None, "feed", times, None), P(), P()),
        out_specs=P("feed", times, None),
        check_vma=False,
    )

    def run(voltages, channel_lag, offsets):
        return body(jnp.asarray(high), jnp.asarray(rest), voltages, channel_lag, offsets)

    return run
```

profile of v0, /device:TPU:1, one launch (start us, length us, event | category | flops | bytes accessed | tf_op | source)
XLA Modules:
  0.0 107.0 jit_solution(14480549482717307016)
XLA Ops:
  0.0 1.8 %copy.11 = bf16[2,8,4,8192]{3,1,0,2:T(8,128)(2,1)S(1)} copy(bf16[2,8,4,8192]{3,2,1,0:T(4,128)(2,1)} %param.5) | data formatting | bytes 2097152 | tf_op args[0]
  1.8 1.6 %pack.1 = bf16[256,16,128]{2,1,0:T(8,128)(2,1)S(1)} custom-call(bf16[4,16,8192]{2,1,0:T(8,128)(2,1)S(1)} %bitcast.17), custom_call_target="tpu_custom_call" | custom-call | tf_op jit(solution)/shard_map/pack/pallas_call | solution.py:217
  3.4 0.0 copy-start
  3.4 0.0 copy-start.1
  3.4 53.4 %all_to_all.10 = bf16[256,16,128]{2,1,0:T(8,128)(2,1)S(1)} all-to-all(bf16[256,16,128]{2,1,0:T(8,128)(2,1)S(1)} %pack.1), channel_id=1, replica_groups=mesh['feed'=32,'y'=8,'core'=2] {'feed','y'}, dimensions={0} | all-to-all | bytes 2097152 | tf_op jit(solution)/shard_map/all_to_all | solution.py:226
  56.9 0.0 copy-done
  56.9 0.0 copy-done.1
  56.9 0.0 copy-start.3
  56.9 2.2 %beams.1.own_ref = bf16[8,128,128]{2,1,0:T(8,128)(2,1)S(1)} custom-call(bf16[512,512]{1,0:T(8,128)(2,1)S(1)} %copy-done.1, bf16[512,512]{1,0:T(8,128)(2,1)S(1)} %copy-done, bf16[32,8,16,128]{3,2,1,0:T(8,128)(2,1)S(1)} %bitcast.16), custom_call_target="tpu_custom_call" | custom-call | tf_op jit(solution)/shard_map/beams/pallas_call | solution.py:241
  59.1 4.7 %collective-permute-start = (bf16[8,128,128]{2,1,0:T(8,128)(2,1)S(1)}, bf16[8,128,128]{2,1,0:T(8,128)(2,1)S(1)}, u32[]{:S(2)}, u32[]{:S(2)}) collective-permute-start(bf16[8,128,128]{2,1,0:T(8,128)(2,1)S(1)} %beams.1.own_ref), channel_id=1, source_target_pairs={{0,1},{1,0},{2,3},{3,2},{4,5},{5,4},{6,7},{7,6},{8,9},{9,8},{10,11... | collective-permute-start | bytes 786440 | tf_op jit(solution)/shard_map/ppermute | solution.py:254
  63.8 0.0 copy-done.3
  63.8 0.7 copy.12
  64.4 1.7 %masks.1.mask_ref = f32[6,8,128]{2,1,0:T(8,128)} custom-call(s32[1]{0:T(128)} %bitcast.1.place_ref, s32[64,128]{1,0:T(8,128)} %bitcast.23, s32[5,32,128]{2,1,0:T(8,128)} %bitcast.21), custom_call_target="tpu_custom_call" | custom-call | tf_op jit(solution)/shard_map/masks/pallas_call | solution.py:229
  66.1 0.0 collective-permute-done.other_ref
  66.1 0.0 copy-start.2
  66.1 0.7 copy-done.2
  66.9 7.8 %tree.1 = f32[32,8,4,128]{3,2,1,0:T(4,128)S(1)} custom-call(s32[1]{0:T(128)} %bitcast.core_ref, f32[6,8,128]{2,1,0:T(8,128)S(1)} %copy-done.2, bf16[8,128,128]{2,1,0:T(8,128)(2,1)S(1)} %beams.1.own_ref, bf16[8,128,128]{2,1,0:T(8,128)(2,1)S(1)} %collective-permute-done.other_ref), custom_call_target="tpu_custom_call" | custom-call | tf_op jit(solution)/shard_map/tree/pallas_call | solution.py:257
  74.7 29.6 %all_to_all.11 = f32[256,4,128]{2,1,0:T(4,128)S(1)} all-to-all(f32[256,4,128]{2,1,0:T(4,128)S(1)} %bitcast.18), channel_id=1, replica_groups=mesh['feed'=32,'y'=8,'core'=2] {'feed','y'}, dimensions={0} | all-to-all | bytes 1048576 | tf_op jit(solution)/shard_map/all_to_all | solution.py:266
  104.3 1.5 %unpack.1 = f32[2,8,8192]{2,1,0:T(8,128)S(1)} custom-call(f32[128,8,128]{2,1,0:T(8,128)S(1)} %bitcast.19), custom_call_target="tpu_custom_call" | custom-call | tf_op jit(solution)/shard_map/unpack/pallas_call | solution.py:268
  105.8 1.2 %copy.7 = f32[8,2,8192]{2,1,0:T(2,128)} copy(f32[8,2,8192]{2,0,1:T(8,128)S(1)} %bitcast.20) | data formatting | bytes 1048576 | tf_op jit(solution)/shard_map/transpose | solution.py:277
Async XLA Ops:
  3.4 53.5 %copy-start = (bf16[512,512]{1,0:T(8,128)(2,1)S(1)}, bf16[512,512]{1,0:T(8,128)(2,1)}, u32[]{:S(2)}) copy-start(bf16[512,512]{1,0:T(8,128)(2,1)} %constant.21.clone.rest_ref) | copy-start | bytes 1572868
  3.4 53.5 %copy-start.1 = (bf16[512,512]{1,0:T(8,128)(2,1)S(1)}, bf16[512,512]{1,0:T(8,128)(2,1)}, u32[]{:S(2)}) copy-start(bf16[512,512]{1,0:T(8,128)(2,1)} %constant.20.clone.high_ref) | copy-start | bytes 1572868
  56.9 6.9 %copy-start.3 = (s32[5,4096]{1,0:T(8,128)S(1)}, s32[5,4096]{1,0:T(8,128)}, u32[]{:S(2)}) copy-start(s32[5,4096]{1,0:T(8,128)} %param.7) | copy-start | bytes 245764
  59.1 7.0 %collective-permute-start = (bf16[8,128,128]{2,1,0:T(8,128)(2,1)S(1)}, bf16[8,128,128]{2,1,0:T(8,128)(2,1)S(1)}, u32[]{:S(2)}, u32[]{:S(2)}) collective-permute-start(bf16[8,128,128]{2,1,0:T(8,128)(2,1)S(1)} %beams.1.own_ref), channel_id=1, source_target_pairs={{0,1},{1,0},{2,3},{3,2},{4,5},{5,4},{6,7},{7,6},{8,9},{9,8},{10,11... | collective-permute-start | bytes 786440 | tf_op jit(solution)/shard_map/ppermute | solution.py:254
  66.1 0.7 copy-start.2
where the time goes:
time: 107 us
  blocking collectives  83 us (78%)
  Pallas kernels  14.8 us (14%)
  starting transfers between devices  4.66 us (4%)
  local copies, waits for them, and re-layouts  4.41 us (4%)
    all_to_all x1, blocking collectives, on_device(): lax.all_to_all(packed, ('feed', 'y'), split_axis=0, concat_axis=0, tiled=...  53.4 us
    all_to_all x1, blocking collectives, on_device(): lax.all_to_all(trials, ('feed', 'y'), split_axis=0, concat_axis=0, tiled=...  29.6 us
    pallas_call x1, Pallas kernels, on_device(): pl.pallas_call(tree_kernel, in_specs=[smem, vmem, vmem, vmem], out_specs=...  7.8 us
    ppermute x1, starting transfers between devices, on_device(): other = lax.ppermute(own, 'core', [(0, 1), (1, 0)])  4.66 us
    unnamed x10, local copies, waits for them, and re-layouts  3.21 us
    pallas_call x1, Pallas kernels, on_device(): pl.pallas_call(beam_kernel, grid=(y_count // several,), in_specs=[pl.Bloc...  2.19 us
  transfers between devices with their start and end apart: 1, of which 0 were waited for; matrix products, arithmetic and copies ran while one was open for 1% of the time, Pallas kernels for 2%

commit v1 on v0

v1 whole, which is shorter than its diff:
```python
import functools
import math

import jax
import jax.numpy as jnp
import ml_dtypes
import numpy as np
from jax import lax
from jax.experimental import pallas as pl
from jax.experimental.pallas import tpu as pltpu
from jax.sharding import Mesh
from jax.sharding import PartitionSpec as P

DS = 2
SECTIONS = 5
GROUP = 2**SECTIONS
LANES = 128
TOP = 14.5
FINE = 800.0
KNEE = -66.0
COARSE = 16.0
KNEE_CODE = (KNEE - TOP) * FINE + 65535.0
VMEM_LIMIT = 48 * 1024 * 1024


def dft_tables(feeds):
    hi, big, low = np.meshgrid(np.arange(4), np.arange(feeds // 8), np.arange(2), indexing="ij")
    beam = (8 * big + 2 * hi + low).reshape(-1)
    feed = np.arange(feeds)
    angle = (beam[:, None] * feed[None, :] % feeds) * (2.0 * math.pi / feeds)
    cosine = np.cos(angle) / math.sqrt(feeds)
    sine = np.sin(angle) / math.sqrt(feeds)
    real = np.stack([cosine.reshape(feeds, -1, 8), sine.reshape(feeds, -1, 8)], axis=2)
    imag = np.stack([-sine.reshape(feeds, -1, 8), cosine.reshape(feeds, -1, 8)], axis=2)
    table = np.concatenate([real, imag], axis=0).reshape(2 * feeds, 2 * feeds)
    high = table.astype(ml_dtypes.bfloat16)
    rest = (table - high.astype(np.float64)).astype(ml_dtypes.bfloat16)
    return high, rest


def lane_index(shape):
    return lax.broadcasted_iota(jnp.int32, shape, len(shape) - 1)


def roll(x, by):
    return pltpu.roll(x, by % x.shape[-1], x.ndim - 1)


def swap_blocks(rows):
    lane = lane_index(rows[0].shape)
    low_half = lane < 64
    even = lane % 64 < 32
    mid = [None] * 4
    for n in range(2):
        mid[n] = jnp.where(low_half, rows[n], roll(rows[n + 2], 64))
        mid[n + 2] = jnp.where(low_half, roll(rows[n], 64), rows[n + 2])
    out = [None] * 4
    for n in (0, 2):
        out[n] = jnp.where(even, mid[n], roll(mid[n + 1], 32))
        out[n + 1] = jnp.where(even, roll(mid[n], -32), mid[n + 1])
    return out


def encode(x):
    level = jnp.log2(jnp.maximum(x, 2.0**-126))
    fine = (level - TOP) * FINE + 65535.0
    coarse = (level - KNEE) * COARSE + KNEE_CODE
    code = jnp.floor(jnp.maximum(fine, coarse) + 0.5).astype(jnp.int32)
    return jnp.where(x > 0.0, code, 0)


def decode(code):
    value = code.astype(jnp.float32)
    fine = (value - 65535.0) * (1.0 / FINE) + TOP
    coarse = (value - KNEE_CODE) * (1.0 / COARSE) + KNEE
    return jnp.where(code > 0, jnp.exp2(jnp.minimum(fine, coarse)), 0.0)


def pack_kernel(x_ref, out_ref):
    tiles = x_ref.shape[2] // LANES

    def step(j, _):
        lanes = pl.ds(pl.multiple_of(j * LANES, LANES), LANES)
        rows = [x_ref[n, :, lanes].astype(jnp.float32) for n in range(4)]
        for g, value in enumerate(swap_blocks(rows)):
            out_ref[4 * j + g] = value.astype(jnp.bfloat16)
        return 0

    lax.fori_loop(0, tiles, step, 0, unroll=4)


def beam_kernel(high_ref, rest_ref, x_ref, out_ref):
    sources, blocks, cf, lanes = x_ref.shape
    several = 2
    feeds = high_ref.shape[0] // 2
    rows = feeds // 4
    lane = lane_index((rows, lanes))
    even = lane % 64 < 32
    low_half = lane < 64
    for y in range(0, blocks, several):
        x = jnp.concatenate(
            [x_ref[:, y + k].reshape(sources * cf, lanes) for k in range(several)], axis=1
        )
        beam = jnp.dot(high_ref[...], x, preferred_element_type=jnp.float32)
        beam = beam + jnp.dot(rest_ref[...], x, preferred_element_type=jnp.float32)
        power = beam[:feeds] * beam[:feeds] + beam[feeds:] * beam[feeds:]
        for k in range(several):
            p = [
                power[g * rows : (g + 1) * rows, k * lanes : (k + 1) * lanes] for g in range(4)
            ]
            pairs = [
                jnp.where(even, p[g] + roll(p[g], -32), p[g + 1] + roll(p[g + 1], 32))
                for g in (0, 2)
            ]
            first = jnp.where(low_half, pairs[0], roll(pairs[1], 64))
            second = jnp.where(low_half, roll(pairs[0], 64), pairs[1])
            out_ref[2 * (y + k)] = (first * (1.0 / DS)).astype(jnp.bfloat16)
            out_ref[2 * (y + k) + 1] = (second * (1.0 / DS)).astype(jnp.bfloat16)


def tree_kernel(place_ref, core_ref, lag_ref, off_ref, own_ref, other_ref, out_ref):
    count = own_ref.shape[0]
    times = 2 * count
    rows = 8
    lane = lane_index((rows, LANES))
    channel = lane % GROUP
    place = place_ref[0]

    per_lag = LANES // GROUP
    lag = jnp.broadcast_to(lag_ref[pl.ds(place // per_lag, 1), :], (rows, LANES))
    lag = jnp.take_along_axis(lag, (place % per_lag) * GROUP + channel, axis=1)
    half_group = GROUP // 2
    per_off = LANES // half_group
    start = pl.multiple_of(place // per_off * LANES, LANES)
    uppers, takes, partners = [], [], []
    for s in range(SECTIONS):
        h = 2**s
        values = jnp.broadcast_to(off_ref[pl.ds(s, 1), pl.ds(start, LANES)], (rows, LANES))
        pair = h * (channel // (2 * h)) + channel % h
        off = jnp.take_along_axis(values, (place % per_off) * half_group + pair, axis=1)
        upper = (channel // h) % 2 == 1
        uppers.append(upper)
        takes.append(jnp.logical_and(upper, off == 1))
        partners.append(jnp.where(upper, lane - h, lane + h))

    zero = jnp.zeros((rows, LANES), jnp.float32)

    def back(level, t, by):
        return level[t - by] if t >= by else zero

    def run(is_odd):
        def step(k, _):
            at = pl.ds(pl.multiple_of(k * 2 * rows, 2 * rows), 2 * rows)
            for q in range(2):
                level = []
                for t in range(times):
                    mine = (t // 2) % 2 == (1 if is_odd else 0)
                    source = own_ref if mine else other_ref
                    block = source[t // 4 * 2 + t % 2, at, :].astype(jnp.float32)
                    level.append(block[q * rows : (q + 1) * rows])
                level = [
                    jnp.where(
                        lag == 0,
                        level[t],
                        jnp.where(lag == 1, back(level, t, 1), back(level, t, 2)),
                    )
                    for t in range(times)
                ]
                for s in range(SECTIONS):
                    after = []
                    for t in range(times):
                        mine = (t // 2) % 2 == (1 if is_odd else 0)
                        if s == SECTIONS - 1 and not mine:
                            after.append(None)
                            continue
                        one, two = back(level, t, 1), back(level, t, 2)
                        sent = jnp.where(takes[s], one, level[t])
                        kept = jnp.where(takes[s], two, jnp.where(uppers[s], one, level[t]))
                        after.append(kept + jnp.take_along_axis(sent, partners[s], axis=1))
                    level = after
                scale = 1.0 / 2**SECTIONS
                for y in range(count // 2):
                    t = 4 * y + (2 if is_odd else 0)
                    word = encode(level[t] * scale) | (encode(level[t + 1] * scale) << 16)
                    for i in range(rows // 2):
                        out_ref[(2 * k + q) * (rows // 2) + i, y] = word[2 * i : 2 * i + 2]
            return 0

        lax.fori_loop(0, own_ref.shape[1] // (2 * rows), step, 0)

    @pl.when(core_ref[0] == 0)
    def _():
        run(False)

    @pl.when(core_ref[0] != 0)
    def _():
        run(True)


def unpack_kernel(x_ref, out_ref):
    tiles = x_ref.shape[0]
    lane = lane_index((8, LANES))
    row = lax.broadcasted_iota(jnp.int32, (8, LANES), 0)
    stay_far = (row < 4) == (lane < 64)
    low_row = row % 4 < 2
    stay_near = low_row == (lane % 64 < 32)

    def step(j, _):
        v = x_ref[j]
        u = jnp.where(stay_far, v, roll(pltpu.roll(v, 4, 0), 64))
        moved = jnp.where(
            low_row, roll(pltpu.roll(u, 6, 0), 32), roll(pltpu.roll(u, 2, 0), -32)
        )
        w = jnp.where(stay_near, u, moved)
        lanes = pl.ds(pl.multiple_of(j * LANES, LANES), LANES)
        out_ref[0, :, lanes] = decode(w & 65535)
        out_ref[1, :, lanes] = decode((w >> 16) & 65535)
        return 0

    lax.fori_loop(0, tiles, step, 0, unroll=4)


def on_device(high, rest, voltages, channel_lag, offsets):
    parts, local, samp, channels = voltages.shape
    feed_count = lax.axis_size("feed")
    y_count = lax.axis_size("y")
    peers = feed_count * y_count
    cf = parts * local
    params = pltpu.CompilerParams(vmem_limit_bytes=VMEM_LIMIT)
    vmem = pl.BlockSpec(memory_space=pltpu.VMEM)
    smem = pl.BlockSpec(memory_space=pltpu.SMEM)

    def call(kernel, name, shape, dtype, specs, *operands):
        return pl.pallas_call(
            kernel,
            in_specs=specs,
            out_specs=vmem,
            out_shape=jax.ShapeDtypeStruct(shape, dtype),
            compiler_params=params,
            name=name,
        )(*operands)

    rows = voltages.reshape(cf, samp, channels).transpose(1, 0, 2)
    packed = call(pack_kernel, "pack", (peers, cf, LANES), jnp.bfloat16, [vmem], rows)
    turned = lax.all_to_all(packed, ("feed", "y"), split_axis=0, concat_axis=0, tiled=True)
    turned = turned.reshape(feed_count, y_count, cf, LANES)
    beams = feed_count * local
    own = call(
        beam_kernel,
        "beams",
        (2 * y_count, beams // 4, LANES),
        jnp.bfloat16,
        [vmem] * 3,
        high,
        rest,
        turned,
    )
    other = lax.ppermute(own, "core", [(0, 1), (1, 0)])
    place = (lax.axis_index("feed") * y_count + lax.axis_index("y")).reshape(1)
    core = lax.axis_index("core").reshape(1)
    codes = call(
        tree_kernel,
        "tree",
        (feed_count, y_count, 2, LANES),
        jnp.int32,
        [smem, smem] + [vmem] * 4,
        place,
        core,
        channel_lag.reshape(-1, LANES),
        offsets,
        own,
        other,
    ).reshape(peers, 2, LANES)
    back = lax.all_to_all(codes, ("feed", "y"), split_axis=0, concat_axis=0, tiled=True)
    out = call(
        unpack_kernel,
        "unpack",
        (2, 8, channels),
        jnp.float32,
        [vmem],
        back.reshape(peers // 4, 8, LANES),
    )
    return out.transpose(1, 0, 2)


def solution(mesh):
    devices = mesh.devices
    fine = Mesh(devices.reshape(devices.shape[0], -1, 2), ("feed", "y", "core"))
    high, rest = dft_tables(8 * devices.shape[0])
    times = ("y", "core")
    body = jax.shard_map(
        functools.partial(on_device),
        mesh=fine,
        in_specs=(P(), P(), P(None, "feed", times, None), P(), P()),
        out_specs=P("feed", times, None),
        check_vma=False,
    )

    def run(voltages, channel_lag, offsets):
        return body(jnp.asarray(high), jnp.asarray(rest), voltages, channel_lag, offsets)

    return run
```

time: 107 us -> 94.7 us (0.89)
  Pallas kernels: 14.8 us -> 8.66 us
  blocking collectives: 83 us -> 76.9 us
  local copies, waits for them, and re-layouts: 4.41 us -> 3.02 us
  waiting for transfers between devices: 0.01 us -> 1.13 us
    pallas_call x5 -> x4, Pallas kernels: 14.8 us -> 8.66 us  [call(): pl.pallas_call(kernel, in_specs=specs, out_specs=vmem, out_shape=jax.Shap...]
    all_to_all x1, blocking collectives: 29.6 us -> 23.5 us  [on_device(): lax.all_to_all(codes, ('feed', 'y'), split_axis=0, concat_axis=0, tiled=T...]
    unnamed x10 -> x9, local copies, waits for them, and re-layouts: 3.21 us -> 1.82 us
    ppermute x1, waiting for transfers between devices: 0.01 us -> 1.13 us  [on_device(): other = lax.ppermute(own, 'core', [(0, 1), (1, 0)])]
  transfers between devices with their start and end apart: 1 -> 1, of which waited for: 0 -> 1; matrix products, arithmetic and copies ran while one was open for 1% -> 0% of each run, Pallas kernels for 2% -> 0%
where the time goes in v1:
time: 94.7 us; the launch traced here: 94.5 us
  blocking collectives  76.9 us (81%)
  Pallas kernels  8.66 us (9%)
  starting transfers between devices  4.66 us (5%)
  local copies, waits for them, and re-layouts  3.02 us (3%)
  waiting for transfers between devices  1.13 us (1%)
    all_to_all x1, blocking collectives, on_device(): lax.all_to_all(packed, ('feed', 'y'), split_axis=0, concat_axis=0, tiled=...  53.4 us
    all_to_all x1, blocking collectives, on_device(): lax.all_to_all(codes, ('feed', 'y'), split_axis=0, concat_axis=0, tiled=T...  23.5 us
    pallas_call x4, Pallas kernels, call(): pl.pallas_call(kernel, in_specs=specs, out_specs=vmem, out_shape=jax.Shap...  8.66 us
    ppermute x1, starting transfers between devices, on_device(): other = lax.ppermute(own, 'core', [(0, 1), (1, 0)])  4.66 us
  transfers between devices with their start and end apart: 1, of which 1 were waited for; matrix products, arithmetic and copies ran while one was open for 0% of the time, Pallas kernels for 0%

profile of v1, /device:TPU:1, one launch (start us, length us, event | category | flops | bytes accessed | tf_op | source)
XLA Modules:
  0.0 94.5 jit_solution(7619816313594565339)
XLA Ops:
  0.0 1.8 %copy.9 = bf16[2,8,4,8192]{3,1,0,2:T(8,128)(2,1)S(1)} copy(bf16[2,8,4,8192]{3,2,1,0:T(4,128)(2,1)} %param.5) | data formatting | bytes 2097152 | tf_op args[0]
  1.8 2.6 %pack.1 = bf16[256,16,128]{2,1,0:T(8,128)(2,1)S(1)} custom-call(bf16[4,16,8192]{2,1,0:T(8,128)(2,1)S(1)} %bitcast.13), custom_call_target="tpu_custom_call" | custom-call | tf_op jit(solution)/shard_map/pack/pallas_call | solution.py:234
  4.4 0.0 copy-start
  4.4 0.0 copy-start.1
  4.4 53.4 %all_to_all.10 = bf16[256,16,128]{2,1,0:T(8,128)(2,1)S(1)} all-to-all(bf16[256,16,128]{2,1,0:T(8,128)(2,1)S(1)} %pack.1), channel_id=1, replica_groups=mesh['feed'=32,'y'=8,'core'=2] {'feed','y'}, dimensions={0} | all-to-all | bytes 2097152 | tf_op jit(solution)/shard_map/all_to_all | solution.py:245
  57.9 0.0 copy-done
  57.9 0.0 copy-done.1
  57.9 0.0 copy-start.2
  57.9 0.0 copy-start.3
  57.9 1.5 %beams.1.own_ref = bf16[16,64,128]{2,1,0:T(8,128)(2,1)S(1)} custom-call(bf16[512,512]{1,0:T(8,128)(2,1)S(1)} %copy-done.1, bf16[512,512]{1,0:T(8,128)(2,1)S(1)} %copy-done, bf16[32,8,16,128]{3,2,1,0:T(8,128)(2,1)S(1)} %bitcast.12), custom_call_target="tpu_custom_call" | custom-call | tf_op jit(solution)/shard_map/beams/pallas_call | solution.py:234
  59.4 4.7 %collective-permute-start = (bf16[16,64,128]{2,1,0:T(8,128)(2,1)S(1)}, bf16[16,64,128]{2,1,0:T(8,128)(2,1)S(1)}, u32[]{:S(2)}, u32[]{:S(2)}) collective-permute-start(bf16[16,64,128]{2,1,0:T(8,128)(2,1)S(1)} %beams.1.own_ref), channel_id=1, source_target_pairs={{0,1},{1,0},{2,3},{3,2},{4,5},{5,4},{6,7},{7,6},{8,9},{9,8},{10,11... | collective-permute-start | bytes 786440 | tf_op jit(solution)/shard_map/ppermute | solution.py:258
  64.0 1.1 %collective-permute-done.other_ref = bf16[16,64,128]{2,1,0:T(8,128)(2,1)S(1)} collective-permute-done((bf16[16,64,128]{2,1,0:T(8,128)(2,1)S(1)}, bf16[16,64,128]{2,1,0:T(8,128)(2,1)S(1)}, u32[]{:S(2)}, u32[]{:S(2)}) %collective-permute-start) | collective-permute-done | bytes 262176 | tf_op jit(solution)/shard_map/ppermute | solution.py:258
  65.2 0.0 copy-done.2
  65.2 0.0 copy-done.3
  65.2 2.0 %tree.1 = s32[32,8,2,128]{3,2,1,0:T(2,128)S(1)} custom-call(s32[1]{0:T(128)} %bitcast.place_ref, s32[1]{0:T(128)} %bitcast.1.core_ref, s32[64,128]{1,0:T(8,128)S(1)} %bitcast.17, s32[5,4096]{1,0:T(8,128)S(1)} %copy-done.2, bf16[16,64,128]{2,1,0:T(8,128)(2,1)S(1)} %beams.1.own_ref, bf16[16,64,128]{2,1,0:T(8,128)(2,1)S(1)} %collective-permute-done.other_ref), custom_call_target="tpu_custom_call" | custom-call | tf_op jit(solution)/shard_map/tree/pallas_call | solution.py:234
  67.2 23.5 %all_to_all.11 = s32[256,2,128]{2,1,0:T(2,128)S(1)} all-to-all(s32[256,2,128]{2,1,0:T(2,128)S(1)} %bitcast.15), channel_id=1, replica_groups=mesh['feed'=32,'y'=8,'core'=2] {'feed','y'}, dimensions={0} | all-to-all | bytes 524288 | tf_op jit(solution)/shard_map/all_to_all | solution.py:274
  90.7 2.6 %unpack.1 = f32[2,8,8192]{2,1,0:T(8,128)S(1)} custom-call(s32[64,8,128]{2,1,0:T(8,128)S(1)} %bitcast.16), custom_call_target="tpu_custom_call" | custom-call | tf_op jit(solution)/shard_map/unpack/pallas_call | solution.py:234
  93.3 1.2 %copy.7 = f32[8,2,8192]{2,1,0:T(2,128)} copy(f32[8,2,8192]{2,0,1:T(8,128)S(1)} %bitcast.14) | data formatting | bytes 1048576 | tf_op jit(solution)/shard_map/transpose | solution.py:283
Async XLA Ops:
  4.4 53.5 %copy-start = (bf16[512,512]{1,0:T(8,128)(2,1)S(1)}, bf16[512,512]{1,0:T(8,128)(2,1)}, u32[]{:S(2)}) copy-start(bf16[512,512]{1,0:T(8,128)(2,1)} %constant.21.clone.rest_ref) | copy-start | bytes 1572868
  4.4 53.5 %copy-start.1 = (bf16[512,512]{1,0:T(8,128)(2,1)S(1)}, bf16[512,512]{1,0:T(8,128)(2,1)}, u32[]{:S(2)}) copy-start(bf16[512,512]{1,0:T(8,128)(2,1)} %constant.20.clone.high_ref) | copy-start | bytes 1572868
  57.9 7.3 %copy-start.2 = (s32[5,4096]{1,0:T(8,128)S(1)}, s32[5,4096]{1,0:T(8,128)}, u32[]{:S(2)}) copy-start(s32[5,4096]{1,0:T(8,128)} %off_ref.1) | copy-start | bytes 245764
  57.9 7.3 %copy-start.3 = (s32[8192]{0:T(1024)S(1)}, s32[8192]{0:T(1024)}, u32[]{:S(2)}) copy-start(s32[8192]{0:T(1024)} %param.6) | copy-start | bytes 98308
  59.4 5.8 %collective-permute-start = (bf16[16,64,128]{2,1,0:T(8,128)(2,1)S(1)}, bf16[16,64,128]{2,1,0:T(8,128)(2,1)S(1)}, u32[]{:S(2)}, u32[]{:S(2)}) collective-permute-start(bf16[16,64,128]{2,1,0:T(8,128)(2,1)S(1)} %beams.1.own_ref), channel_id=1, source_target_pairs={{0,1},{1,0},{2,3},{3,2},{4,5},{5,4},{6,7},{7,6},{8,9},{9,8},{10,11... | collective-permute-start | bytes 786440 | tf_op jit(solution)/shard_map/ppermute | solution.py:258

commit v2 on v1

--- a/solution.py
+++ b/solution.py
@@ -50,14 +50,16 @@
     lane = lane_index(rows[0].shape)
     low_half = lane < 64
     even = lane % 64 < 32
-    mid = [None] * 4
-    for n in range(2):
-        mid[n] = jnp.where(low_half, rows[n], roll(rows[n + 2], 64))
-        mid[n + 2] = jnp.where(low_half, roll(rows[n], 64), rows[n + 2])
-    out = [None] * 4
-    for n in (0, 2):
-        out[n] = jnp.where(even, mid[n], roll(mid[n + 1], 32))
-        out[n + 1] = jnp.where(even, roll(mid[n], -32), mid[n + 1])
+    turned = [rows[0]] + [roll(rows[n], 32 * n) for n in range(1, 4)]
+    out = []
+    for g in range(4):
+        blocks = [turned[(m - g) % 4] for m in range(4)]
+        mixed = jnp.where(
+            low_half,
+            jnp.where(even, blocks[0], blocks[1]),
+            jnp.where(even, blocks[2], blocks[3]),
+        )
+        out.append(roll(mixed, -32 * g) if g else mixed)
     return out
 
 
@@ -81,12 +83,12 @@
 
     def step(j, _):
         lanes = pl.ds(pl.multiple_of(j * LANES, LANES), LANES)
-        rows = [x_ref[n, :, lanes].astype(jnp.float32) for n in range(4)]
+        rows = [x_ref[n, :, lanes] for n in range(4)]
         for g, value in enumerate(swap_blocks(rows)):
-            out_ref[4 * j + g] = value.astype(jnp.bfloat16)
+            out_ref[4 * j + g] = value
         return 0
 
-    lax.fori_loop(0, tiles, step, 0, unroll=4)
+    lax.fori_loop(0, tiles, step, 0, unroll=16)
 
 
 def beam_kernel(high_ref, rest_ref, x_ref, out_ref):
@@ -213,11 +215,13 @@
         )
         w = jnp.where(stay_near, u, moved)
         lanes = pl.ds(pl.multiple_of(j * LANES, LANES), LANES)
-        out_ref[0, :, lanes] = decode(w & 65535)
-        out_ref[1, :, lanes] = decode((w >> 16) & 65535)
+        for k in range(2):
+            twice = jnp.take_along_axis(w, row // 2 + 4 * k, axis=0)
+            value = decode(jnp.where(row % 2 == 1, twice >> 16, twice) & 65535)
+            out_ref[4 * k : 4 * k + 4, :, lanes] = value.reshape(4, 2, LANES)
         return 0
 
-    lax.fori_loop(0, tiles, step, 0, unroll=4)
+    lax.fori_loop(0, tiles, step, 0, unroll=16)
 
 
 def on_device(high, rest, voltages, channel_lag, offsets):
@@ -272,15 +276,14 @@
         other,
     ).reshape(peers, 2, LANES)
     back = lax.all_to_all(codes, ("feed", "y"), split_axis=0, concat_axis=0, tiled=True)
-    out = call(
+    return call(
         unpack_kernel,
         "unpack",
-        (2, 8, channels),
+        (8, 2, channels),
         jnp.float32,
         [vmem],
         back.reshape(peers // 4, 8, LANES),
     )
-    return out.transpose(1, 0, 2)
 
 
 def solution(mesh):

time: 94.7 us -> 91 us (0.961)
  Pallas kernels: 8.66 us -> 6.11 us
  local copies, waits for them, and re-layouts: 3.02 us -> 1.82 us
    pallas_call x4, Pallas kernels: 8.66 us -> 6.11 us  [call(): pl.pallas_call(kernel, in_specs=specs, out_specs=vmem, out_shape=jax.Shap...]
    transpose x1 -> x0, local copies, waits for them, and re-layouts: 1.2 us -> none  [on_device(): return out.transpose(1, 0, 2)]
where the time goes in v2:
time: 91 us; the launch traced here: 90.7 us
  blocking collectives  76.9 us (85%)
  Pallas kernels  6.11 us (7%)
  starting transfers between devices  4.66 us (5%)
  local copies, waits for them, and re-layouts  1.82 us (2%)
  waiting for transfers between devices  1.13 us (1%)
    all_to_all x1, blocking collectives, on_device(): lax.all_to_all(packed, ('feed', 'y'), split_axis=0, concat_axis=0, tiled=...  53.4 us
    all_to_all x1, blocking collectives, on_device(): lax.all_to_all(codes, ('feed', 'y'), split_axis=0, concat_axis=0, tiled=T...  23.5 us
    pallas_call x4, Pallas kernels, call(): pl.pallas_call(kernel, in_specs=specs, out_specs=vmem, out_shape=jax.Shap...  6.11 us
    ppermute x1, starting transfers between devices, on_device(): other = lax.ppermute(own, 'core', [(0, 1), (1, 0)])  4.66 us
    unnamed x9, local copies, waits for them, and re-layouts  1.82 us
  transfers between devices with their start and end apart: 1, of which 1 were waited for; matrix products, arithmetic and copies ran while one was open for 0% of the time, Pallas kernels for 0%

profile of v2, /device:TPU:1, one launch (start us, length us, event | category | flops | bytes accessed | tf_op | source)
XLA Modules:
  0.0 90.7 jit_solution(8757260323117606344)
XLA Ops:
  0.0 1.8 %copy.8 = bf16[2,8,4,8192]{3,1,0,2:T(8,128)(2,1)S(1)} copy(bf16[2,8,4,8192]{3,2,1,0:T(4,128)(2,1)} %param.5) | data formatting | bytes 2097152 | tf_op args[0]
  1.8 0.8 pack.1
  2.7 0.0 copy-start
  2.7 0.0 copy-start.1
  2.7 53.4 %all_to_all.10 = bf16[256,16,128]{2,1,0:T(8,128)(2,1)S(1)} all-to-all(bf16[256,16,128]{2,1,0:T(8,128)(2,1)S(1)} %pack.1), channel_id=1, replica_groups=mesh['feed'=32,'y'=8,'core'=2] {'feed','y'}, dimensions={0} | all-to-all | bytes 2097152 | tf_op jit(solution)/shard_map/all_to_all | solution.py:249
  56.1 0.0 copy-done
  56.1 0.0 copy-done.1
  56.1 0.0 copy-start.2
  56.1 0.0 copy-start.3
  56.2 1.5 %beams.1.own_ref = bf16[16,64,128]{2,1,0:T(8,128)(2,1)S(1)} custom-call(bf16[512,512]{1,0:T(8,128)(2,1)S(1)} %copy-done.1, bf16[512,512]{1,0:T(8,128)(2,1)S(1)} %copy-done, bf16[32,8,16,128]{3,2,1,0:T(8,128)(2,1)S(1)} %bitcast.11), custom_call_target="tpu_custom_call" | custom-call | tf_op jit(solution)/shard_map/beams/pallas_call | solution.py:238
  57.6 4.7 %collective-permute-start = (bf16[16,64,128]{2,1,0:T(8,128)(2,1)S(1)}, bf16[16,64,128]{2,1,0:T(8,128)(2,1)S(1)}, u32[]{:S(2)}, u32[]{:S(2)}) collective-permute-start(bf16[16,64,128]{2,1,0:T(8,128)(2,1)S(1)} %beams.1.own_ref), channel_id=1, source_target_pairs={{0,1},{1,0},{2,3},{3,2},{4,5},{5,4},{6,7},{7,6},{8,9},{9,8},{10,11... | collective-permute-start | bytes 786440 | tf_op jit(solution)/shard_map/ppermute | solution.py:262
  62.3 1.1 %collective-permute-done.other_ref = bf16[16,64,128]{2,1,0:T(8,128)(2,1)S(1)} collective-permute-done((bf16[16,64,128]{2,1,0:T(8,128)(2,1)S(1)}, bf16[16,64,128]{2,1,0:T(8,128)(2,1)S(1)}, u32[]{:S(2)}, u32[]{:S(2)}) %collective-permute-start) | collective-permute-done | bytes 262176 | tf_op jit(solution)/shard_map/ppermute | solution.py:262
  63.4 0.0 copy-done.2
  63.4 0.0 copy-done.3
  63.4 2.0 %tree.1 = s32[32,8,2,128]{3,2,1,0:T(2,128)S(1)} custom-call(s32[1]{0:T(128)} %bitcast.place_ref, s32[1]{0:T(128)} %bitcast.1.core_ref, s32[64,128]{1,0:T(8,128)S(1)} %bitcast.15, s32[5,4096]{1,0:T(8,128)S(1)} %copy-done.2, bf16[16,64,128]{2,1,0:T(8,128)(2,1)S(1)} %beams.1.own_ref, bf16[16,64,128]{2,1,0:T(8,128)(2,1)S(1)} %collective-permute-done.other_ref), custom_call_target="tpu_custom_call" | custom-call | tf_op jit(solution)/shard_map/tree/pallas_call | solution.py:238
  65.5 23.5 %all_to_all.11 = s32[256,2,128]{2,1,0:T(2,128)S(1)} all-to-all(s32[256,2,128]{2,1,0:T(2,128)S(1)} %bitcast.13), channel_id=1, replica_groups=mesh['feed'=32,'y'=8,'core'=2] {'feed','y'}, dimensions={0} | all-to-all | bytes 524288 | tf_op jit(solution)/shard_map/all_to_all | solution.py:278
  88.9 1.8 %unpack.1 = f32[8,2,8192]{2,1,0:T(2,128)} custom-call(s32[64,8,128]{2,1,0:T(8,128)S(1)} %bitcast.14), custom_call_target="tpu_custom_call" | custom-call | tf_op jit(solution)/shard_map/unpack/pallas_call | solution.py:238
Async XLA Ops:
  2.7 53.5 %copy-start = (bf16[512,512]{1,0:T(8,128)(2,1)S(1)}, bf16[512,512]{1,0:T(8,128)(2,1)}, u32[]{:S(2)}) copy-start(bf16[512,512]{1,0:T(8,128)(2,1)} %constant.21.clone.rest_ref) | copy-start | bytes 1572868
  2.7 53.5 %copy-start.1 = (bf16[512,512]{1,0:T(8,128)(2,1)S(1)}, bf16[512,512]{1,0:T(8,128)(2,1)}, u32[]{:S(2)}) copy-start(bf16[512,512]{1,0:T(8,128)(2,1)} %constant.20.clone.high_ref) | copy-start | bytes 1572868
  56.1 7.3 %copy-start.2 = (s32[5,4096]{1,0:T(8,128)S(1)}, s32[5,4096]{1,0:T(8,128)}, u32[]{:S(2)}) copy-start(s32[5,4096]{1,0:T(8,128)} %off_ref.1) | copy-start | bytes 245764
  56.1 7.3 %copy-start.3 = (s32[8192]{0:T(1024)S(1)}, s32[8192]{0:T(1024)}, u32[]{:S(2)}) copy-start(s32[8192]{0:T(1024)} %param.6) | copy-start | bytes 98308
  57.6 5.8 %collective-permute-start = (bf16[16,64,128]{2,1,0:T(8,128)(2,1)S(1)}, bf16[16,64,128]{2,1,0:T(8,128)(2,1)S(1)}, u32[]{:S(2)}, u32[]{:S(2)}) collective-permute-start(bf16[16,64,128]{2,1,0:T(8,128)(2,1)S(1)} %beams.1.own_ref), channel_id=1, source_target_pairs={{0,1},{1,0},{2,3},{3,2},{4,5},{5,4},{6,7},{7,6},{8,9},{9,8},{10,11... | collective-permute-start | bytes 786440 | tf_op jit(solution)/shard_map/ppermute | solution.py:262

commit v3 on v2

--- a/solution.py
+++ b/solution.py
@@ -246,7 +246,7 @@
 
     rows = voltages.reshape(cf, samp, channels).transpose(1, 0, 2)
     packed = call(pack_kernel, "pack", (peers, cf, LANES), jnp.bfloat16, [vmem], rows)
-    turned = lax.all_to_all(packed, ("feed", "y"), split_axis=0, concat_axis=0, tiled=True)
+    turned = lax.all_to_all(packed, "feed", split_axis=0, concat_axis=0, tiled=True)
     turned = turned.reshape(feed_count, y_count, cf, LANES)
     beams = feed_count * local
     own = call(
@@ -259,6 +259,7 @@
         rest,
         turned,
     )
+    own = lax.all_to_all(own, "y", split_axis=0, concat_axis=0, tiled=True)
     other = lax.ppermute(own, "core", [(0, 1), (1, 0)])
     place = (lax.axis_index("feed") * y_count + lax.axis_index("y")).reshape(1)
     core = lax.axis_index("core").reshape(1)

time: 91 us -> 95.6 us (1.051)
  blocking collectives: 76.9 us -> 80.1 us
  starting transfers between devices: 4.66 us -> 6.04 us
    all_to_all x1 -> x2, blocking collectives: 53.4 us -> 56.1 us  [the longest x1 39.9 us: on_device(): lax.all_to_all(packed, 'feed', split_axis=0, concat_axis=0, tiled=True)]
    ppermute x1, starting transfers between devices: 4.66 us -> 6.04 us  [on_device(): other = lax.ppermute(own, 'core', [(0, 1), (1, 0)])]
where the time goes in v3:
time: 95.6 us; the launch traced here: 95.3 us
  blocking collectives  80.1 us (84%)
  Pallas kernels  6.11 us (6%)
  starting transfers between devices  6.04 us (6%)
  local copies, waits for them, and re-layouts  1.83 us (2%)
  waiting for transfers between devices  1.13 us (1%)
    all_to_all x1, blocking collectives, on_device(): lax.all_to_all(packed, 'feed', split_axis=0, concat_axis=0, tiled=True)  39.9 us
    all_to_all x1, blocking collectives, on_device(): lax.all_to_all(codes, ('feed', 'y'), split_axis=0, concat_axis=0, tiled=T...  24 us
    all_to_all x1, blocking collectives, on_device(): own = lax.all_to_all(own, 'y', split_axis=0, concat_axis=0, tiled=True)  16.2 us
    pallas_call x4, Pallas kernels, call(): pl.pallas_call(kernel, in_specs=specs, out_specs=vmem, out_shape=jax.Shap...  6.11 us
    ppermute x1, starting transfers between devices, on_device(): other = lax.ppermute(own, 'core', [(0, 1), (1, 0)])  6.04 us
  transfers between devices with their start and end apart: 1, of which 1 were waited for; matrix products, arithmetic and copies ran while one was open for 0% of the time, Pallas kernels for 0%

profile of v3, /device:TPU:1, one launch (start us, length us, event | category | flops | bytes accessed | tf_op | source)
XLA Modules:
  0.0 95.3 jit_solution(15472860556531871560)
XLA Ops:
  0.0 1.8 %copy.8 = bf16[2,8,4,8192]{3,1,0,2:T(8,128)(2,1)S(1)} copy(bf16[2,8,4,8192]{3,2,1,0:T(4,128)(2,1)} %param.5) | data formatting | bytes 2097152 | tf_op args[0]
  1.8 0.8 pack.1
  2.7 0.0 copy-start
  2.7 0.0 copy-start.1
  2.7 39.9 %all_to_all.15 = bf16[256,16,128]{2,1,0:T(8,128)(2,1)S(1)} all-to-all(bf16[256,16,128]{2,1,0:T(8,128)(2,1)S(1)} %pack.1), channel_id=1, replica_groups=mesh['feed'=32,'y'=8,'core'=2] {'feed'}, dimensions={0} | all-to-all | bytes 2097152 | tf_op jit(solution)/shard_map/all_to_all | solution.py:249
  42.5 0.0 copy-done
  42.5 0.0 copy-done.1
  42.5 1.5 %beams.1 = bf16[16,64,128]{2,1,0:T(8,128)(2,1)S(1)} custom-call(bf16[512,512]{1,0:T(8,128)(2,1)S(1)} %copy-done.1, bf16[512,512]{1,0:T(8,128)(2,1)S(1)} %copy-done, bf16[32,8,16,128]{3,2,1,0:T(8,128)(2,1)S(1)} %bitcast.11), custom_call_target="tpu_custom_call" | custom-call | tf_op jit(solution)/shard_map/beams/pallas_call | solution.py:238
  44.0 0.0 copy-start.2
  44.0 0.0 copy-start.3
  44.0 16.2 %all_to_all.16.own_ref = bf16[16,64,128]{2,1,0:T(8,128)(2,1)S(1)} all-to-all(bf16[16,64,128]{2,1,0:T(8,128)(2,1)S(1)} %beams.1), channel_id=1, replica_groups=mesh['feed'=32,'y'=8,'core'=2] {'y'}, dimensions={0} | all-to-all | bytes 524288 | tf_op jit(solution)/shard_map/all_to_all | solution.py:262
  60.2 6.0 %collective-permute-start = (bf16[16,64,128]{2,1,0:T(8,128)(2,1)S(1)}, bf16[16,64,128]{2,1,0:T(8,128)(2,1)S(1)}, u32[]{:S(2)}, u32[]{:S(2)}) collective-permute-start(bf16[16,64,128]{2,1,0:T(8,128)(2,1)S(1)} %all_to_all.16.own_ref), channel_id=1, source_target_pairs={{0,1},{1,0},{2,3},{3,2},{4,5},{5,4},{6,7},{7,6},{8,9},{9,8},{10,11... | collective-permute-start | bytes 786440 | tf_op jit(solution)/shard_map/ppermute | solution.py:263
  66.3 1.1 %collective-permute-done.other_ref = bf16[16,64,128]{2,1,0:T(8,128)(2,1)S(1)} collective-permute-done((bf16[16,64,128]{2,1,0:T(8,128)(2,1)S(1)}, bf16[16,64,128]{2,1,0:T(8,128)(2,1)S(1)}, u32[]{:S(2)}, u32[]{:S(2)}) %collective-permute-start) | collective-permute-done | bytes 262176 | tf_op jit(solution)/shard_map/ppermute | solution.py:263
  67.4 0.0 copy-done.2
  67.4 0.0 copy-done.3
  67.4 2.0 %tree.1 = s32[32,8,2,128]{3,2,1,0:T(2,128)S(1)} custom-call(s32[1]{0:T(128)} %bitcast.place_ref, s32[1]{0:T(128)} %bitcast.1.core_ref, s32[64,128]{1,0:T(8,128)S(1)} %bitcast.15, s32[5,4096]{1,0:T(8,128)S(1)} %copy-done.2, bf16[16,64,128]{2,1,0:T(8,128)(2,1)S(1)} %all_to_all.16.own_ref, bf16[16,64,128]{2,1,0:T(8,128)(2,1)S(1)} %collective-permute-done.other_ref), custom_call_target="tpu_custom_call" | custom-call | tf_op jit(solution)/shard_map/tree/pallas_call | solution.py:238
  69.5 24.0 %all_to_all.17 = s32[256,2,128]{2,1,0:T(2,128)S(1)} all-to-all(s32[256,2,128]{2,1,0:T(2,128)S(1)} %bitcast.13), channel_id=1, replica_groups=mesh['feed'=32,'y'=8,'core'=2] {'feed','y'}, dimensions={0} | all-to-all | bytes 524288 | tf_op jit(solution)/shard_map/all_to_all | solution.py:279
  93.5 1.8 %unpack.1 = f32[8,2,8192]{2,1,0:T(2,128)} custom-call(s32[64,8,128]{2,1,0:T(8,128)S(1)} %bitcast.14), custom_call_target="tpu_custom_call" | custom-call | tf_op jit(solution)/shard_map/unpack/pallas_call | solution.py:238
Async XLA Ops:
  2.7 39.9 %copy-start = (bf16[512,512]{1,0:T(8,128)(2,1)S(1)}, bf16[512,512]{1,0:T(8,128)(2,1)}, u32[]{:S(2)}) copy-start(bf16[512,512]{1,0:T(8,128)(2,1)} %constant.21.clone.rest_ref) | copy-start | bytes 1572868
  2.7 39.9 %copy-start.1 = (bf16[512,512]{1,0:T(8,128)(2,1)S(1)}, bf16[512,512]{1,0:T(8,128)(2,1)}, u32[]{:S(2)}) copy-start(bf16[512,512]{1,0:T(8,128)(2,1)} %constant.20.clone.high_ref) | copy-start | bytes 1572868
  44.0 23.4 %copy-start.2 = (s32[5,4096]{1,0:T(8,128)S(1)}, s32[5,4096]{1,0:T(8,128)}, u32[]{:S(2)}) copy-start(s32[5,4096]{1,0:T(8,128)} %off_ref.1) | copy-start | bytes 245764
  44.0 23.4 %copy-start.3 = (s32[8192]{0:T(1024)S(1)}, s32[8192]{0:T(1024)}, u32[]{:S(2)}) copy-start(s32[8192]{0:T(1024)} %param.6) | copy-start | bytes 98308
  60.2 7.2 %collective-permute-start = (bf16[16,64,128]{2,1,0:T(8,128)(2,1)S(1)}, bf16[16,64,128]{2,1,0:T(8,128)(2,1)S(1)}, u32[]{:S(2)}, u32[]{:S(2)}) collective-permute-start(bf16[16,64,128]{2,1,0:T(8,128)(2,1)S(1)} %all_to_all.16.own_ref), channel_id=1, source_target_pairs={{0,1},{1,0},{2,3},{3,2},{4,5},{5,4},{6,7},{7,6},{8,9},{9,8},{10,11... | collective-permute-start | bytes 786440 | tf_op jit(solution)/shard_map/ppermute | solution.py:263

commit v4 on v2

--- a/solution.py
+++ b/solution.py
@@ -20,6 +20,8 @@
 KNEE = -66.0
 COARSE = 16.0
 KNEE_CODE = (KNEE - TOP) * FINE + 65535.0
+LEAST = -126.0
+LEAST_CODE = int((LEAST - KNEE) * COARSE + KNEE_CODE)
 VMEM_LIMIT = 48 * 1024 * 1024
 
 
@@ -64,18 +66,17 @@
 
 
 def encode(x):
-    level = jnp.log2(jnp.maximum(x, 2.0**-126))
-    fine = (level - TOP) * FINE + 65535.0
-    coarse = (level - KNEE) * COARSE + KNEE_CODE
-    code = jnp.floor(jnp.maximum(fine, coarse) + 0.5).astype(jnp.int32)
-    return jnp.where(x > 0.0, code, 0)
+    level = jnp.log2(jnp.maximum(x, 2.0**LEAST))
+    fine = level * FINE + (65535.5 - TOP * FINE)
+    coarse = level * COARSE + (KNEE_CODE + 0.5 - KNEE * COARSE)
+    return jnp.maximum(fine, coarse).astype(jnp.int32)
 
 
 def decode(code):
     value = code.astype(jnp.float32)
-    fine = (value - 65535.0) * (1.0 / FINE) + TOP
-    coarse = (value - KNEE_CODE) * (1.0 / COARSE) + KNEE
-    return jnp.where(code > 0, jnp.exp2(jnp.minimum(fine, coarse)), 0.0)
+    fine = value * (1.0 / FINE) + (TOP - 65535.0 / FINE)
+    coarse = value * (1.0 / COARSE) + (KNEE - KNEE_CODE / COARSE)
+    return jnp.where(code > LEAST_CODE, jnp.exp2(jnp.minimum(fine, coarse)), 0.0)
 
 
 def pack_kernel(x_ref, out_ref):
@@ -147,8 +148,10 @@
 
     zero = jnp.zeros((rows, LANES), jnp.float32)
 
-    def back(level, t, by):
-        return level[t - by] if t >= by else zero
+    def delay(level, late):
+        return [
+            jnp.where(late, level[t - 1] if t else zero, level[t]) for t in range(times)
+        ]
 
     def run(is_odd):
         def step(k, _):
@@ -160,25 +163,17 @@
                     source = own_ref if mine else other_ref
                     block = source[t // 4 * 2 + t % 2, at, :].astype(jnp.float32)
                     level.append(block[q * rows : (q + 1) * rows])
-                level = [
-                    jnp.where(
-                        lag == 0,
-                        level[t],
-                        jnp.where(lag == 1, back(level, t, 1), back(level, t, 2)),
-                    )
-                    for t in range(times)
-                ]
+                level = delay(delay(level, lag >= 1), lag >= 2)
                 for s in range(SECTIONS):
+                    sent = delay(level, takes[s])
                     after = []
                     for t in range(times):
                         mine = (t // 2) % 2 == (1 if is_odd else 0)
                         if s == SECTIONS - 1 and not mine:
                             after.append(None)
                             continue
-                        one, two = back(level, t, 1), back(level, t, 2)
-                        sent = jnp.where(takes[s], one, level[t])
-                        kept = jnp.where(takes[s], two, jnp.where(uppers[s], one, level[t]))
-                        after.append(kept + jnp.take_along_axis(sent, partners[s], axis=1))
+                        kept = jnp.where(uppers[s], sent[t - 1] if t else zero, level[t])
+                        after.append(kept + jnp.take_along_axis(sent[t], partners[s], axis=1))
                     level = after
                 scale = 1.0 / 2**SECTIONS
                 for y in range(count // 2):
@@ -221,7 +216,7 @@
             out_ref[4 * k : 4 * k + 4, :, lanes] = value.reshape(4, 2, LANES)
         return 0
 
-    lax.fori_loop(0, tiles, step, 0, unroll=16)
+    lax.fori_loop(0, tiles, step, 0, unroll=32)
 
 
 def on_device(high, rest, voltages, channel_lag, offsets):

time: 91 us -> 90.5 us (level)
  no operation moved by 1% of the time
where the time goes in v4:
time: 90.5 us; the launch traced here: 90.2 us
  blocking collectives  76.9 us (85%)
  Pallas kernels  5.62 us (6%)
  starting transfers between devices  4.66 us (5%)
  local copies, waits for them, and re-layouts  1.82 us (2%)
  waiting for transfers between devices  1.13 us (1%)
    all_to_all x1, blocking collectives, on_device(): lax.all_to_all(packed, ('feed', 'y'), split_axis=0, concat_axis=0, tiled=...  53.4 us
    all_to_all x1, blocking collectives, on_device(): lax.all_to_all(codes, ('feed', 'y'), split_axis=0, concat_axis=0, tiled=T...  23.5 us
    pallas_call x4, Pallas kernels, call(): pl.pallas_call(kernel, in_specs=specs, out_specs=vmem, out_shape=jax.Shap...  5.62 us
    ppermute x1, starting transfers between devices, on_device(): other = lax.ppermute(own, 'core', [(0, 1), (1, 0)])  4.66 us
    unnamed x9, local copies, waits for them, and re-layouts  1.82 us
  transfers between devices with their start and end apart: 1, of which 1 were waited for; matrix products, arithmetic and copies ran while one was open for 0% of the time, Pallas kernels for 0%

profile of v4, /device:TPU:1, one launch (start us, length us, event | category | flops | bytes accessed | tf_op | source)
XLA Modules:
  0.0 90.2 jit_solution(15814970553502512383)
XLA Ops:
  0.0 1.8 %copy.8 = bf16[2,8,4,8192]{3,1,0,2:T(8,128)(2,1)S(1)} copy(bf16[2,8,4,8192]{3,2,1,0:T(4,128)(2,1)} %param.5) | data formatting | bytes 2097152 | tf_op args[0]
  1.8 0.8 pack.1
  2.7 0.0 copy-start
  2.7 0.0 copy-start.1
  2.7 53.4 %all_to_all.10 = bf16[256,16,128]{2,1,0:T(8,128)(2,1)S(1)} all-to-all(bf16[256,16,128]{2,1,0:T(8,128)(2,1)S(1)} %pack.1), channel_id=1, replica_groups=mesh['feed'=32,'y'=8,'core'=2] {'feed','y'}, dimensions={0} | all-to-all | bytes 2097152 | tf_op jit(solution)/shard_map/all_to_all | solution.py:244
  56.1 0.0 copy-done
  56.1 0.0 copy-done.1
  56.1 0.0 copy-start.2
  56.1 0.0 copy-start.3
  56.2 1.5 %beams.1.own_ref = bf16[16,64,128]{2,1,0:T(8,128)(2,1)S(1)} custom-call(bf16[512,512]{1,0:T(8,128)(2,1)S(1)} %copy-done.1, bf16[512,512]{1,0:T(8,128)(2,1)S(1)} %copy-done, bf16[32,8,16,128]{3,2,1,0:T(8,128)(2,1)S(1)} %bitcast.11), custom_call_target="tpu_custom_call" | custom-call | tf_op jit(solution)/shard_map/beams/pallas_call | solution.py:233
  57.6 4.7 %collective-permute-start = (bf16[16,64,128]{2,1,0:T(8,128)(2,1)S(1)}, bf16[16,64,128]{2,1,0:T(8,128)(2,1)S(1)}, u32[]{:S(2)}, u32[]{:S(2)}) collective-permute-start(bf16[16,64,128]{2,1,0:T(8,128)(2,1)S(1)} %beams.1.own_ref), channel_id=1, source_target_pairs={{0,1},{1,0},{2,3},{3,2},{4,5},{5,4},{6,7},{7,6},{8,9},{9,8},{10,11... | collective-permute-start | bytes 786440 | tf_op jit(solution)/shard_map/ppermute | solution.py:257
  62.3 1.1 %collective-permute-done.other_ref = bf16[16,64,128]{2,1,0:T(8,128)(2,1)S(1)} collective-permute-done((bf16[16,64,128]{2,1,0:T(8,128)(2,1)S(1)}, bf16[16,64,128]{2,1,0:T(8,128)(2,1)S(1)}, u32[]{:S(2)}, u32[]{:S(2)}) %collective-permute-start) | collective-permute-done | bytes 262176 | tf_op jit(solution)/shard_map/ppermute | solution.py:257
  63.4 0.0 copy-done.2
  63.4 0.0 copy-done.3
  63.4 1.9 %tree.1 = s32[32,8,2,128]{3,2,1,0:T(2,128)S(1)} custom-call(s32[1]{0:T(128)} %bitcast.place_ref, s32[1]{0:T(128)} %bitcast.1.core_ref, s32[64,128]{1,0:T(8,128)S(1)} %bitcast.15, s32[5,4096]{1,0:T(8,128)S(1)} %copy-done.2, bf16[16,64,128]{2,1,0:T(8,128)(2,1)S(1)} %beams.1.own_ref, bf16[16,64,128]{2,1,0:T(8,128)(2,1)S(1)} %collective-permute-done.other_ref), custom_call_target="tpu_custom_call" | custom-call | tf_op jit(solution)/shard_map/tree/pallas_call | solution.py:233
  65.3 23.5 %all_to_all.11 = s32[256,2,128]{2,1,0:T(2,128)S(1)} all-to-all(s32[256,2,128]{2,1,0:T(2,128)S(1)} %bitcast.13), channel_id=1, replica_groups=mesh['feed'=32,'y'=8,'core'=2] {'feed','y'}, dimensions={0} | all-to-all | bytes 524288 | tf_op jit(solution)/shard_map/all_to_all | solution.py:273
  88.8 1.4 %unpack.1 = f32[8,2,8192]{2,1,0:T(2,128)} custom-call(s32[64,8,128]{2,1,0:T(8,128)S(1)} %bitcast.14), custom_call_target="tpu_custom_call" | custom-call | tf_op jit(solution)/shard_map/unpack/pallas_call | solution.py:233
Async XLA Ops:
  2.7 53.5 %copy-start = (bf16[512,512]{1,0:T(8,128)(2,1)S(1)}, bf16[512,512]{1,0:T(8,128)(2,1)}, u32[]{:S(2)}) copy-start(bf16[512,512]{1,0:T(8,128)(2,1)} %constant.21.clone.rest_ref) | copy-start | bytes 1572868
  2.7 53.5 %copy-start.1 = (bf16[512,512]{1,0:T(8,128)(2,1)S(1)}, bf16[512,512]{1,0:T(8,128)(2,1)}, u32[]{:S(2)}) copy-start(bf16[512,512]{1,0:T(8,128)(2,1)} %constant.20.clone.high_ref) | copy-start | bytes 1572868
  56.1 7.3 %copy-start.2 = (s32[5,4096]{1,0:T(8,128)S(1)}, s32[5,4096]{1,0:T(8,128)}, u32[]{:S(2)}) copy-start(s32[5,4096]{1,0:T(8,128)} %off_ref.1) | copy-start | bytes 245764
  56.1 7.3 %copy-start.3 = (s32[8192]{0:T(1024)S(1)}, s32[8192]{0:T(1024)}, u32[]{:S(2)}) copy-start(s32[8192]{0:T(1024)} %param.6) | copy-start | bytes 98308
  57.6 5.8 %collective-permute-start = (bf16[16,64,128]{2,1,0:T(8,128)(2,1)S(1)}, bf16[16,64,128]{2,1,0:T(8,128)(2,1)S(1)}, u32[]{:S(2)}, u32[]{:S(2)}) collective-permute-start(bf16[16,64,128]{2,1,0:T(8,128)(2,1)S(1)} %beams.1.own_ref), channel_id=1, source_target_pairs={{0,1},{1,0},{2,3},{3,2},{4,5},{5,4},{6,7},{7,6},{8,9},{9,8},{10,11... | collective-permute-start | bytes 786440 | tf_op jit(solution)/shard_map/ppermute | solution.py:257

commit v5 on v4

--- a/solution.py
+++ b/solution.py
@@ -111,12 +111,14 @@
             p = [
                 power[g * rows : (g + 1) * rows, k * lanes : (k + 1) * lanes] for g in range(4)
             ]
-            pairs = [
-                jnp.where(even, p[g] + roll(p[g], -32), p[g + 1] + roll(p[g + 1], 32))
-                for g in (0, 2)
-            ]
-            first = jnp.where(low_half, pairs[0], roll(pairs[1], 64))
-            second = jnp.where(low_half, roll(pairs[0], 64), pairs[1])
+            pairs = []
+            for g in (0, 2):
+                crossed = jnp.where(even, p[g + 1], p[g])
+                crossed = jnp.take_along_axis(crossed, lane ^ 32, axis=1)
+                pairs.append(jnp.where(even, p[g], p[g + 1]) + crossed)
+            crossed = roll(jnp.where(low_half, pairs[1], pairs[0]), 64)
+            first = jnp.where(low_half, pairs[0], crossed)
+            second = jnp.where(low_half, crossed, pairs[1])
             out_ref[2 * (y + k)] = (first * (1.0 / DS)).astype(jnp.bfloat16)
             out_ref[2 * (y + k) + 1] = (second * (1.0 / DS)).astype(jnp.bfloat16)
 
@@ -199,15 +201,13 @@
     lane = lane_index((8, LANES))
     row = lax.broadcasted_iota(jnp.int32, (8, LANES), 0)
     stay_far = (row < 4) == (lane < 64)
-    low_row = row % 4 < 2
-    stay_near = low_row == (lane % 64 < 32)
+    stay_near = (row % 4 < 2) == (lane % 64 < 32)
 
     def step(j, _):
         v = x_ref[j]
         u = jnp.where(stay_far, v, roll(pltpu.roll(v, 4, 0), 64))
-        moved = jnp.where(
-            low_row, roll(pltpu.roll(u, 6, 0), 32), roll(pltpu.roll(u, 2, 0), -32)
-        )
+        moved = jnp.take_along_axis(u, row ^ 2, axis=0)
+        moved = jnp.take_along_axis(moved, lane ^ 32, axis=1)
         w = jnp.where(stay_near, u, moved)
         lanes = pl.ds(pl.multiple_of(j * LANES, LANES), LANES)
         for k in range(2):

time: 90.5 us -> 90.4 us (level)
  no operation moved by 1% of the time
where the time goes in v5:
time: 90.4 us; the launch traced here: 90.2 us
  blocking collectives  76.9 us (85%)
  Pallas kernels  5.59 us (6%)
  starting transfers between devices  4.66 us (5%)
  local copies, waits for them, and re-layouts  1.82 us (2%)
  waiting for transfers between devices  1.13 us (1%)
    all_to_all x1, blocking collectives, on_device(): lax.all_to_all(packed, ('feed', 'y'), split_axis=0, concat_axis=0, tiled=...  53.4 us
    all_to_all x1, blocking collectives, on_device(): lax.all_to_all(codes, ('feed', 'y'), split_axis=0, concat_axis=0, tiled=T...  23.5 us
    pallas_call x4, Pallas kernels, call(): pl.pallas_call(kernel, in_specs=specs, out_specs=vmem, out_shape=jax.Shap...  5.59 us
    ppermute x1, starting transfers between devices, on_device(): other = lax.ppermute(own, 'core', [(0, 1), (1, 0)])  4.66 us
    unnamed x9, local copies, waits for them, and re-layouts  1.82 us
  transfers between devices with their start and end apart: 1, of which 1 were waited for; matrix products, arithmetic and copies ran while one was open for 0% of the time, Pallas kernels for 0%

profile of v5, /device:TPU:1, one launch (start us, length us, event | category | flops | bytes accessed | tf_op | source)
XLA Modules:
  0.0 90.2 jit_solution(8299726020807230360)
XLA Ops:
  0.0 1.8 %copy.8 = bf16[2,8,4,8192]{3,1,0,2:T(8,128)(2,1)S(1)} copy(bf16[2,8,4,8192]{3,2,1,0:T(4,128)(2,1)} %param.5) | data formatting | bytes 2097152 | tf_op args[0]
  1.8 0.8 pack.1
  2.7 0.0 copy-start
  2.7 0.0 copy-start.1
  2.7 53.4 %all_to_all.10 = bf16[256,16,128]{2,1,0:T(8,128)(2,1)S(1)} all-to-all(bf16[256,16,128]{2,1,0:T(8,128)(2,1)S(1)} %pack.1), channel_id=1, replica_groups=mesh['feed'=32,'y'=8,'core'=2] {'feed','y'}, dimensions={0} | all-to-all | bytes 2097152 | tf_op jit(solution)/shard_map/all_to_all | solution.py:244
  56.1 0.0 copy-done
  56.1 0.0 copy-done.1
  56.1 0.0 copy-start.2
  56.1 0.0 copy-start.3
  56.2 1.4 %beams.1.own_ref = bf16[16,64,128]{2,1,0:T(8,128)(2,1)S(1)} custom-call(bf16[512,512]{1,0:T(8,128)(2,1)S(1)} %copy-done.1, bf16[512,512]{1,0:T(8,128)(2,1)S(1)} %copy-done, bf16[32,8,16,128]{3,2,1,0:T(8,128)(2,1)S(1)} %bitcast.11), custom_call_target="tpu_custom_call" | custom-call | tf_op jit(solution)/shard_map/beams/pallas_call | solution.py:233
  57.6 4.7 %collective-permute-start = (bf16[16,64,128]{2,1,0:T(8,128)(2,1)S(1)}, bf16[16,64,128]{2,1,0:T(8,128)(2,1)S(1)}, u32[]{:S(2)}, u32[]{:S(2)}) collective-permute-start(bf16[16,64,128]{2,1,0:T(8,128)(2,1)S(1)} %beams.1.own_ref), channel_id=1, source_target_pairs={{0,1},{1,0},{2,3},{3,2},{4,5},{5,4},{6,7},{7,6},{8,9},{9,8},{10,11... | collective-permute-start | bytes 786440 | tf_op jit(solution)/shard_map/ppermute | solution.py:257
  62.2 1.1 %collective-permute-done.other_ref = bf16[16,64,128]{2,1,0:T(8,128)(2,1)S(1)} collective-permute-done((bf16[16,64,128]{2,1,0:T(8,128)(2,1)S(1)}, bf16[16,64,128]{2,1,0:T(8,128)(2,1)S(1)}, u32[]{:S(2)}, u32[]{:S(2)}) %collective-permute-start) | collective-permute-done | bytes 262176 | tf_op jit(solution)/shard_map/ppermute | solution.py:257
  63.4 0.0 copy-done.2
  63.4 0.0 copy-done.3
  63.4 1.9 %tree.1 = s32[32,8,2,128]{3,2,1,0:T(2,128)S(1)} custom-call(s32[1]{0:T(128)} %bitcast.place_ref, s32[1]{0:T(128)} %bitcast.1.core_ref, s32[64,128]{1,0:T(8,128)S(1)} %bitcast.15, s32[5,4096]{1,0:T(8,128)S(1)} %copy-done.2, bf16[16,64,128]{2,1,0:T(8,128)(2,1)S(1)} %beams.1.own_ref, bf16[16,64,128]{2,1,0:T(8,128)(2,1)S(1)} %collective-permute-done.other_ref), custom_call_target="tpu_custom_call" | custom-call | tf_op jit(solution)/shard_map/tree/pallas_call | solution.py:233
  65.3 23.5 %all_to_all.11 = s32[256,2,128]{2,1,0:T(2,128)S(1)} all-to-all(s32[256,2,128]{2,1,0:T(2,128)S(1)} %bitcast.13), channel_id=1, replica_groups=mesh['feed'=32,'y'=8,'core'=2] {'feed','y'}, dimensions={0} | all-to-all | bytes 524288 | tf_op jit(solution)/shard_map/all_to_all | solution.py:273
  88.7 1.4 %unpack.1 = f32[8,2,8192]{2,1,0:T(2,128)} custom-call(s32[64,8,128]{2,1,0:T(8,128)S(1)} %bitcast.14), custom_call_target="tpu_custom_call" | custom-call | tf_op jit(solution)/shard_map/unpack/pallas_call | solution.py:233
Async XLA Ops:
  2.7 53.5 %copy-start = (bf16[512,512]{1,0:T(8,128)(2,1)S(1)}, bf16[512,512]{1,0:T(8,128)(2,1)}, u32[]{:S(2)}) copy-start(bf16[512,512]{1,0:T(8,128)(2,1)} %constant.21.clone.rest_ref) | copy-start | bytes 1572868
  2.7 53.5 %copy-start.1 = (bf16[512,512]{1,0:T(8,128)(2,1)S(1)}, bf16[512,512]{1,0:T(8,128)(2,1)}, u32[]{:S(2)}) copy-start(bf16[512,512]{1,0:T(8,128)(2,1)} %constant.20.clone.high_ref) | copy-start | bytes 1572868
  56.1 7.2 %copy-start.2 = (s32[5,4096]{1,0:T(8,128)S(1)}, s32[5,4096]{1,0:T(8,128)}, u32[]{:S(2)}) copy-start(s32[5,4096]{1,0:T(8,128)} %off_ref.1) | copy-start | bytes 245764
  56.1 7.2 %copy-start.3 = (s32[8192]{0:T(1024)S(1)}, s32[8192]{0:T(1024)}, u32[]{:S(2)}) copy-start(s32[8192]{0:T(1024)} %param.6) | copy-start | bytes 98308
  57.6 5.8 %collective-permute-start = (bf16[16,64,128]{2,1,0:T(8,128)(2,1)S(1)}, bf16[16,64,128]{2,1,0:T(8,128)(2,1)S(1)}, u32[]{:S(2)}, u32[]{:S(2)}) collective-permute-start(bf16[16,64,128]{2,1,0:T(8,128)(2,1)S(1)} %beams.1.own_ref), channel_id=1, source_target_pairs={{0,1},{1,0},{2,3},{3,2},{4,5},{5,4},{6,7},{7,6},{8,9},{9,8},{10,11... | collective-permute-start | bytes 786440 | tf_op jit(solution)/shard_map/ppermute | solution.py:257

commit v6 on v5

--- a/solution.py
+++ b/solution.py
@@ -93,7 +93,7 @@
 
 
 def beam_kernel(high_ref, rest_ref, x_ref, out_ref):
-    sources, blocks, cf, lanes = x_ref.shape
+    blocks, sources, cf, lanes = x_ref.shape
     several = 2
     feeds = high_ref.shape[0] // 2
     rows = feeds // 4
@@ -102,7 +102,7 @@
     low_half = lane < 64
     for y in range(0, blocks, several):
         x = jnp.concatenate(
-            [x_ref[:, y + k].reshape(sources * cf, lanes) for k in range(several)], axis=1
+            [x_ref[y + k].reshape(sources * cf, lanes) for k in range(several)], axis=1
         )
         beam = jnp.dot(high_ref[...], x, preferred_element_type=jnp.float32)
         beam = beam + jnp.dot(rest_ref[...], x, preferred_element_type=jnp.float32)
@@ -181,8 +181,7 @@
                 for y in range(count // 2):
                     t = 4 * y + (2 if is_odd else 0)
                     word = encode(level[t] * scale) | (encode(level[t + 1] * scale) << 16)
-                    for i in range(rows // 2):
-                        out_ref[(2 * k + q) * (rows // 2) + i, y] = word[2 * i : 2 * i + 2]
+                    out_ref[y, 2 * k + q] = word
             return 0
 
         lax.fori_loop(0, own_ref.shape[1] // (2 * rows), step, 0)
@@ -241,8 +240,8 @@
 
     rows = voltages.reshape(cf, samp, channels).transpose(1, 0, 2)
     packed = call(pack_kernel, "pack", (peers, cf, LANES), jnp.bfloat16, [vmem], rows)
-    turned = lax.all_to_all(packed, ("feed", "y"), split_axis=0, concat_axis=0, tiled=True)
-    turned = turned.reshape(feed_count, y_count, cf, LANES)
+    turned = lax.all_to_all(packed, ("y", "feed"), split_axis=0, concat_axis=0, tiled=True)
+    turned = turned.reshape(y_count, feed_count, cf, LANES)
     beams = feed_count * local
     own = call(
         beam_kernel,
@@ -255,12 +254,12 @@
         turned,
     )
     other = lax.ppermute(own, "core", [(0, 1), (1, 0)])
-    place = (lax.axis_index("feed") * y_count + lax.axis_index("y")).reshape(1)
+    place = (lax.axis_index("y") * feed_count + lax.axis_index("feed")).reshape(1)
     core = lax.axis_index("core").reshape(1)
     codes = call(
         tree_kernel,
         "tree",
-        (feed_count, y_count, 2, LANES),
+        (y_count, feed_count // 4, 8, LANES),
         jnp.int32,
         [smem, smem] + [vmem] * 4,
         place,
@@ -270,7 +269,7 @@
         own,
         other,
     ).reshape(peers, 2, LANES)
-    back = lax.all_to_all(codes, ("feed", "y"), split_axis=0, concat_axis=0, tiled=True)
+    back = lax.all_to_all(codes, ("y", "feed"), split_axis=0, concat_axis=0, tiled=True)
     return call(
         unpack_kernel,
         "unpack",

time: 90.4 us -> 88.8 us (0.982)
  blocking collectives: 76.9 us -> 74.4 us
    all_to_all x2, blocking collectives: 76.9 us -> 74.4 us  [the longest x1 51.5 us: on_device(): lax.all_to_all(packed, ('y', 'feed'), split_axis=0, concat_axis=0, tiled=...]
where the time goes in v6:
time: 88.8 us; the launch traced here: 88 us
  blocking collectives  74.4 us (84%)
  Pallas kernels  5.58 us (6%)
  starting transfers between devices  4.97 us (6%)
  local copies, waits for them, and re-layouts  1.82 us (2%)
  waiting for transfers between devices  1.13 us (1%)
    all_to_all x1, blocking collectives, on_device(): lax.all_to_all(packed, ('y', 'feed'), split_axis=0, concat_axis=0, tiled=...  51.5 us
    all_to_all x1, blocking collectives, on_device(): lax.all_to_all(codes, ('y', 'feed'), split_axis=0, concat_axis=0, tiled=T...  22.9 us
    pallas_call x4, Pallas kernels, call(): pl.pallas_call(kernel, in_specs=specs, out_specs=vmem, out_shape=jax.Shap...  5.58 us
    ppermute x1, starting transfers between devices, on_device(): other = lax.ppermute(own, 'core', [(0, 1), (1, 0)])  4.97 us
    unnamed x9, local copies, waits for them, and re-layouts  1.82 us
  transfers between devices with their start and end apart: 1, of which 1 were waited for; matrix products, arithmetic and copies ran while one was open for 0% of the time, Pallas kernels for 0%

profile of v6, /device:TPU:1, one launch (start us, length us, event | category | flops | bytes accessed | tf_op | source)
XLA Modules:
  0.0 88.0 jit_solution(129351554080081585)
XLA Ops:
  0.0 1.8 %copy.8 = bf16[2,8,4,8192]{3,1,0,2:T(8,128)(2,1)S(1)} copy(bf16[2,8,4,8192]{3,2,1,0:T(4,128)(2,1)} %param.5) | data formatting | bytes 2097152 | tf_op args[0]
  1.8 0.8 pack.1
  2.7 0.0 copy-start
  2.7 0.0 copy-start.1
  2.7 51.5 %all_to_all.10 = bf16[256,16,128]{2,1,0:T(8,128)(2,1)S(1)} all-to-all(bf16[256,16,128]{2,1,0:T(8,128)(2,1)S(1)} %pack.1), channel_id=1, replica_groups=mesh['feed'=32,'y'=8,'core'=2] {'y','feed'}, dimensions={0} | all-to-all | bytes 2097152 | tf_op jit(solution)/shard_map/all_to_all | solution.py:243
  54.2 0.0 copy-done
  54.2 0.0 copy-done.1
  54.2 0.0 copy-start.2
  54.2 0.0 copy-start.3
  54.2 1.4 %beams.1.own_ref = bf16[16,64,128]{2,1,0:T(8,128)(2,1)S(1)} custom-call(bf16[512,512]{1,0:T(8,128)(2,1)S(1)} %copy-done.1, bf16[512,512]{1,0:T(8,128)(2,1)S(1)} %copy-done, bf16[8,32,16,128]{3,2,1,0:T(8,128)(2,1)S(1)} %bitcast.11), custom_call_target="tpu_custom_call" | custom-call | tf_op jit(solution)/shard_map/beams/pallas_call | solution.py:232
  55.6 5.0 %collective-permute-start = (bf16[16,64,128]{2,1,0:T(8,128)(2,1)S(1)}, bf16[16,64,128]{2,1,0:T(8,128)(2,1)S(1)}, u32[]{:S(2)}, u32[]{:S(2)}) collective-permute-start(bf16[16,64,128]{2,1,0:T(8,128)(2,1)S(1)} %beams.1.own_ref), channel_id=1, source_target_pairs={{0,1},{1,0},{2,3},{3,2},{4,5},{5,4},{6,7},{7,6},{8,9},{9,8},{10,11... | collective-permute-start | bytes 786440 | tf_op jit(solution)/shard_map/ppermute | solution.py:256
  60.6 1.1 %collective-permute-done.other_ref = bf16[16,64,128]{2,1,0:T(8,128)(2,1)S(1)} collective-permute-done((bf16[16,64,128]{2,1,0:T(8,128)(2,1)S(1)}, bf16[16,64,128]{2,1,0:T(8,128)(2,1)S(1)}, u32[]{:S(2)}, u32[]{:S(2)}) %collective-permute-start) | collective-permute-done | bytes 262176 | tf_op jit(solution)/shard_map/ppermute | solution.py:256
  61.7 0.0 copy-done.2
  61.7 0.0 copy-done.3
  61.7 1.9 %tree.1 = s32[8,8,8,128]{3,2,1,0:T(8,128)S(1)} custom-call(s32[1]{0:T(128)} %bitcast.place_ref, s32[1]{0:T(128)} %bitcast.1.core_ref, s32[64,128]{1,0:T(8,128)S(1)} %bitcast.15, s32[5,4096]{1,0:T(8,128)S(1)} %copy-done.2, bf16[16,64,128]{2,1,0:T(8,128)(2,1)S(1)} %beams.1.own_ref, bf16[16,64,128]{2,1,0:T(8,128)(2,1)S(1)} %collective-permute-done.other_ref), custom_call_target="tpu_custom_call" | custom-call | tf_op jit(solution)/shard_map/tree/pallas_call | solution.py:232
  63.6 22.9 %all_to_all.11 = s32[256,2,128]{2,1,0:T(2,128)S(1)} all-to-all(s32[256,2,128]{2,1,0:T(2,128)S(1)} %bitcast.13), channel_id=1, replica_groups=mesh['feed'=32,'y'=8,'core'=2] {'y','feed'}, dimensions={0} | all-to-all | bytes 524288 | tf_op jit(solution)/shard_map/all_to_all | solution.py:272
  86.6 1.4 %unpack.1 = f32[8,2,8192]{2,1,0:T(2,128)} custom-call(s32[64,8,128]{2,1,0:T(8,128)S(1)} %bitcast.14), custom_call_target="tpu_custom_call" | custom-call | tf_op jit(solution)/shard_map/unpack/pallas_call | solution.py:232
Async XLA Ops:
  2.7 51.5 %copy-start = (bf16[512,512]{1,0:T(8,128)(2,1)S(1)}, bf16[512,512]{1,0:T(8,128)(2,1)}, u32[]{:S(2)}) copy-start(bf16[512,512]{1,0:T(8,128)(2,1)} %constant.21.clone.rest_ref) | copy-start | bytes 1572868
  2.7 51.5 %copy-start.1 = (bf16[512,512]{1,0:T(8,128)(2,1)S(1)}, bf16[512,512]{1,0:T(8,128)(2,1)}, u32[]{:S(2)}) copy-start(bf16[512,512]{1,0:T(8,128)(2,1)} %constant.20.clone.high_ref) | copy-start | bytes 1572868
  54.2 7.6 %copy-start.2 = (s32[5,4096]{1,0:T(8,128)S(1)}, s32[5,4096]{1,0:T(8,128)}, u32[]{:S(2)}) copy-start(s32[5,4096]{1,0:T(8,128)} %off_ref.1) | copy-start | bytes 245764
  54.2 7.6 %copy-start.3 = (s32[8192]{0:T(1024)S(1)}, s32[8192]{0:T(1024)}, u32[]{:S(2)}) copy-start(s32[8192]{0:T(1024)} %param.6) | copy-start | bytes 98308
  55.6 6.1 %collective-permute-start = (bf16[16,64,128]{2,1,0:T(8,128)(2,1)S(1)}, bf16[16,64,128]{2,1,0:T(8,128)(2,1)S(1)}, u32[]{:S(2)}, u32[]{:S(2)}) collective-permute-start(bf16[16,64,128]{2,1,0:T(8,128)(2,1)S(1)} %beams.1.own_ref), channel_id=1, source_target_pairs={{0,1},{1,0},{2,3},{3,2},{4,5},{5,4},{6,7},{7,6},{8,9},{9,8},{10,11... | collective-permute-start | bytes 786440 | tf_op jit(solution)/shard_map/ppermute | solution.py:256

commit v7 on v6

--- a/solution.py
+++ b/solution.py
@@ -11,6 +11,9 @@
 from jax.sharding import Mesh
 from jax.sharding import PartitionSpec as P
 
+FEED = ("z2", "z1", "z0", "x")
+TIME = ("y2", "y1", "y0", "core")
+PEERS = ("z2", "y2", "z1", "y1", "z0", "y0", "x")
 DS = 2
 SECTIONS = 5
 GROUP = 2**SECTIONS
@@ -38,6 +41,13 @@
     high = table.astype(ml_dtypes.bfloat16)
     rest = (table - high.astype(np.float64)).astype(ml_dtypes.bfloat16)
     return high, rest
+
+
+def woven(z, y):
+    total = 0
+    for bit in range(3):
+        total = total + (z >> bit) % 2 * 2 ** (2 * bit + 1) + (y >> bit) % 2 * 2 ** (2 * bit)
+    return total
 
 
 def lane_index(shape):
@@ -93,7 +103,8 @@
 
 
 def beam_kernel(high_ref, rest_ref, x_ref, out_ref):
-    blocks, sources, cf, lanes = x_ref.shape
+    blocks = 8
+    _, few, cf, lanes = x_ref.shape
     several = 2
     feeds = high_ref.shape[0] // 2
     rows = feeds // 4
@@ -102,7 +113,13 @@
     low_half = lane < 64
     for y in range(0, blocks, several):
         x = jnp.concatenate(
-            [x_ref[y + k].reshape(sources * cf, lanes) for k in range(several)], axis=1
+            [
+                jnp.concatenate(
+                    [x_ref[woven(z, y + k)].reshape(few * cf, lanes) for z in range(8)], axis=0
+                )
+                for k in range(several)
+            ],
+            axis=1,
         )
         beam = jnp.dot(high_ref[...], x, preferred_element_type=jnp.float32)
         beam = beam + jnp.dot(rest_ref[...], x, preferred_element_type=jnp.float32)
@@ -181,7 +198,7 @@
                 for y in range(count // 2):
                     t = 4 * y + (2 if is_odd else 0)
                     word = encode(level[t] * scale) | (encode(level[t + 1] * scale) << 16)
-                    out_ref[y, 2 * k + q] = word
+                    out_ref[woven(2 * k + q, y)] = word
             return 0
 
         lax.fori_loop(0, own_ref.shape[1] // (2 * rows), step, 0)
@@ -220,8 +237,7 @@
 
 def on_device(high, rest, voltages, channel_lag, offsets):
     parts, local, samp, channels = voltages.shape
-    feed_count = lax.axis_size("feed")
-    y_count = lax.axis_size("y")
+    feed_count, y_count = 32, 8
     peers = feed_count * y_count
     cf = parts * local
     params = pltpu.CompilerParams(vmem_limit_bytes=VMEM_LIMIT)
@@ -240,8 +256,8 @@
 
     rows = voltages.reshape(cf, samp, channels).transpose(1, 0, 2)
     packed = call(pack_kernel, "pack", (peers, cf, LANES), jnp.bfloat16, [vmem], rows)
-    turned = lax.all_to_all(packed, ("y", "feed"), split_axis=0, concat_axis=0, tiled=True)
-    turned = turned.reshape(y_count, feed_count, cf, LANES)
+    turned = lax.all_to_all(packed, PEERS, split_axis=0, concat_axis=0, tiled=True)
+    turned = turned.reshape(peers // 4, 4, cf, LANES)
     beams = feed_count * local
     own = call(
         beam_kernel,
@@ -254,12 +270,12 @@
         turned,
     )
     other = lax.ppermute(own, "core", [(0, 1), (1, 0)])
-    place = (lax.axis_index("y") * feed_count + lax.axis_index("feed")).reshape(1)
+    place = lax.axis_index(PEERS).reshape(1)
     core = lax.axis_index("core").reshape(1)
     codes = call(
         tree_kernel,
         "tree",
-        (y_count, feed_count // 4, 8, LANES),
+        (peers // 4, 8, LANES),
         jnp.int32,
         [smem, smem] + [vmem] * 4,
         place,
@@ -269,7 +285,7 @@
         own,
         other,
     ).reshape(peers, 2, LANES)
-    back = lax.all_to_all(codes, ("y", "feed"), split_axis=0, concat_axis=0, tiled=True)
+    back = lax.all_to_all(codes, PEERS, split_axis=0, concat_axis=0, tiled=True)
     return call(
         unpack_kernel,
         "unpack",
@@ -282,14 +298,13 @@
 
 def solution(mesh):
     devices = mesh.devices
-    fine = Mesh(devices.reshape(devices.shape[0], -1, 2), ("feed", "y", "core"))
+    fine = Mesh(devices.reshape((2, 2, 2, 4, 2, 2, 2, 2)), FEED + TIME)
     high, rest = dft_tables(8 * devices.shape[0])
-    times = ("y", "core")
     body = jax.shard_map(
         functools.partial(on_device),
         mesh=fine,
-        in_specs=(P(), P(), P(None, "feed", times, None), P(), P()),
-        out_specs=P("feed", times, None),
+        in_specs=(P(), P(), P(None, FEED, TIME, None), P(), P()),
+        out_specs=P(FEED, TIME, None),
         check_vma=False,
     )
 

time: 88.8 us -> 89.8 us (1.011)
  blocking collectives: 74.4 us -> 76.5 us
    all_to_all x2, blocking collectives: 74.4 us -> 76.5 us  [the longest x1 53.3 us: on_device(): lax.all_to_all(packed, PEERS, split_axis=0, concat_axis=0, tiled=True)]
where the time goes in v7:
time: 89.8 us; the launch traced here: 89.5 us
  blocking collectives  76.5 us (85%)
  Pallas kernels  5.58 us (6%)
  starting transfers between devices  4.39 us (5%)
  local copies, waits for them, and re-layouts  1.83 us (2%)
  waiting for transfers between devices  1.11 us (1%)
    all_to_all x1, blocking collectives, on_device(): lax.all_to_all(packed, PEERS, split_axis=0, concat_axis=0, tiled=True)  53.3 us
    all_to_all x1, blocking collectives, on_device(): back = lax.all_to_all(codes, PEERS, split_axis=0, concat_axis=0, tiled=True)  23.3 us
    pallas_call x4, Pallas kernels, call(): pl.pallas_call(kernel, in_specs=specs, out_specs=vmem, out_shape=jax.Shap...  5.58 us
    ppermute x1, starting transfers between devices, on_device(): other = lax.ppermute(own, 'core', [(0, 1), (1, 0)])  4.39 us
    unnamed x9, local copies, waits for them, and re-layouts  1.83 us
  transfers between devices with their start and end apart: 1, of which 1 were waited for; matrix products, arithmetic and copies ran while one was open for 0% of the time, Pallas kernels for 0%

profile of v7, /device:TPU:1, one launch (start us, length us, event | category | flops | bytes accessed | tf_op | source)
XLA Modules:
  0.0 89.5 jit_solution(12800518432680832316)
XLA Ops:
  0.0 1.8 %copy.8 = bf16[2,8,4,8192]{3,1,0,2:T(8,128)(2,1)S(1)} copy(bf16[2,8,4,8192]{3,2,1,0:T(4,128)(2,1)} %param.5) | data formatting | bytes 2097152 | tf_op args[0]
  1.8 0.8 pack.1
  2.7 0.0 copy-start
  2.7 0.0 copy-start.1
  2.7 53.3 %all_to_all.10 = bf16[256,16,128]{2,1,0:T(8,128)(2,1)S(1)} all-to-all(bf16[256,16,128]{2,1,0:T(8,128)(2,1)S(1)} %pack.1), channel_id=1, replica_groups=mesh['z2'=2,'z1'=2,'z0'=2,'x'=4,'y2'=2,'y1'=2,'y0'=2,'core'=2] {'z2','y2..., dimensions={0} | all-to-all | bytes 2097152 | tf_op jit(solution)/shard_map/all_to_all | solution.py:259
  55.9 0.0 copy-done
  56.0 0.0 copy-done.1
  56.0 0.0 copy-start.2
  56.0 1.4 %beams.1.own_ref = bf16[16,64,128]{2,1,0:T(8,128)(2,1)S(1)} custom-call(bf16[512,512]{1,0:T(8,128)(2,1)S(1)} %copy-done.1, bf16[512,512]{1,0:T(8,128)(2,1)S(1)} %copy-done, bf16[64,4,16,128]{3,2,1,0:T(8,128)(2,1)S(1)} %bitcast.11), custom_call_target="tpu_custom_call" | custom-call | tf_op jit(solution)/shard_map/beams/pallas_call | solution.py:248
  57.4 4.4 %collective-permute-start = (bf16[16,64,128]{2,1,0:T(8,128)(2,1)S(1)}, bf16[16,64,128]{2,1,0:T(8,128)(2,1)S(1)}, u32[]{:S(2)}, u32[]{:S(2)}) collective-permute-start(bf16[16,64,128]{2,1,0:T(8,128)(2,1)S(1)} %beams.1.own_ref), channel_id=1, source_target_pairs={{0,1},{1,0},{2,3},{3,2},{4,5},{5,4},{6,7},{7,6},{8,9},{9,8},{10,11... | collective-permute-start | bytes 786440 | tf_op jit(solution)/shard_map/ppermute | solution.py:272
  61.8 0.0 copy-start.3
  61.8 1.1 %collective-permute-done.other_ref = bf16[16,64,128]{2,1,0:T(8,128)(2,1)S(1)} collective-permute-done((bf16[16,64,128]{2,1,0:T(8,128)(2,1)S(1)}, bf16[16,64,128]{2,1,0:T(8,128)(2,1)S(1)}, u32[]{:S(2)}, u32[]{:S(2)}) %collective-permute-start) | collective-permute-done | bytes 262176 | tf_op jit(solution)/shard_map/ppermute | solution.py:272
  62.9 0.0 copy-done.2
  62.9 0.0 copy-done.3
  62.9 1.9 %tree.1 = s32[64,8,128]{2,1,0:T(8,128)S(1)} custom-call(s32[1]{0:T(128)} %bitcast.place_ref, s32[1]{0:T(128)} %bitcast.1.core_ref, s32[64,128]{1,0:T(8,128)S(1)} %bitcast.15, s32[5,4096]{1,0:T(8,128)S(1)} %copy-done.2, bf16[16,64,128]{2,1,0:T(8,128)(2,1)S(1)} %beams.1.own_ref, bf16[16,64,128]{2,1,0:T(8,128)(2,1)S(1)} %collective-permute-done.other_ref), custom_call_target="tpu_custom_call" | custom-call | tf_op jit(solution)/shard_map/tree/pallas_call | solution.py:248
  64.8 23.3 %all_to_all.11 = s32[256,2,128]{2,1,0:T(2,128)S(1)} all-to-all(s32[256,2,128]{2,1,0:T(2,128)S(1)} %bitcast.13), channel_id=1, replica_groups=mesh['z2'=2,'z1'=2,'z0'=2,'x'=4,'y2'=2,'y1'=2,'y0'=2,'core'=2] {'z2','y2..., dimensions={0} | all-to-all | bytes 524288 | tf_op jit(solution)/shard_map/all_to_all | solution.py:288
  88.1 1.4 %unpack.1 = f32[8,2,8192]{2,1,0:T(2,128)} custom-call(s32[64,8,128]{2,1,0:T(8,128)S(1)} %bitcast.14), custom_call_target="tpu_custom_call" | custom-call | tf_op jit(solution)/shard_map/unpack/pallas_call | solution.py:248
Async XLA Ops:
  2.7 53.3 %copy-start = (bf16[512,512]{1,0:T(8,128)(2,1)S(1)}, bf16[512,512]{1,0:T(8,128)(2,1)}, u32[]{:S(2)}) copy-start(bf16[512,512]{1,0:T(8,128)(2,1)} %constant.47.clone.rest_ref) | copy-start | bytes 1572868
  2.7 53.3 %copy-start.1 = (bf16[512,512]{1,0:T(8,128)(2,1)S(1)}, bf16[512,512]{1,0:T(8,128)(2,1)}, u32[]{:S(2)}) copy-start(bf16[512,512]{1,0:T(8,128)(2,1)} %constant.46.clone.high_ref) | copy-start | bytes 1572868
  56.0 7.0 %copy-start.2 = (s32[5,4096]{1,0:T(8,128)S(1)}, s32[5,4096]{1,0:T(8,128)}, u32[]{:S(2)}) copy-start(s32[5,4096]{1,0:T(8,128)} %off_ref.1) | copy-start | bytes 245764
  57.4 5.5 %collective-permute-start = (bf16[16,64,128]{2,1,0:T(8,128)(2,1)S(1)}, bf16[16,64,128]{2,1,0:T(8,128)(2,1)S(1)}, u32[]{:S(2)}, u32[]{:S(2)}) collective-permute-start(bf16[16,64,128]{2,1,0:T(8,128)(2,1)S(1)} %beams.1.own_ref), channel_id=1, source_target_pairs={{0,1},{1,0},{2,3},{3,2},{4,5},{5,4},{6,7},{7,6},{8,9},{9,8},{10,11... | collective-permute-start | bytes 786440 | tf_op jit(solution)/shard_map/ppermute | solution.py:272
  61.8 1.1 %copy-start.3 = (s32[8192]{0:T(1024)S(1)}, s32[8192]{0:T(1024)}, u32[]{:S(2)}) copy-start(s32[8192]{0:T(1024)} %param.6) | copy-start | bytes 98308

commit v8 on v7

--- a/solution.py
+++ b/solution.py
@@ -11,9 +11,9 @@
 from jax.sharding import Mesh
 from jax.sharding import PartitionSpec as P
 
-FEED = ("z2", "z1", "z0", "x")
-TIME = ("y2", "y1", "y0", "core")
-PEERS = ("z2", "y2", "z1", "y1", "z0", "y0", "x")
+FEED = ("z", "x")
+TIME = ("y", "core")
+PEERS = ("x", "z", "y")
 DS = 2
 SECTIONS = 5
 GROUP = 2**SECTIONS
@@ -41,13 +41,6 @@
     high = table.astype(ml_dtypes.bfloat16)
     rest = (table - high.astype(np.float64)).astype(ml_dtypes.bfloat16)
     return high, rest
-
-
-def woven(z, y):
-    total = 0
-    for bit in range(3):
-        total = total + (z >> bit) % 2 * 2 ** (2 * bit + 1) + (y >> bit) % 2 * 2 ** (2 * bit)
-    return total
 
 
 def lane_index(shape):
@@ -103,8 +96,7 @@
 
 
 def beam_kernel(high_ref, rest_ref, x_ref, out_ref):
-    blocks = 8
-    _, few, cf, lanes = x_ref.shape
+    blocks, lanes = 8, LANES
     several = 2
     feeds = high_ref.shape[0] // 2
     rows = feeds // 4
@@ -115,7 +107,7 @@
         x = jnp.concatenate(
             [
                 jnp.concatenate(
-                    [x_ref[woven(z, y + k)].reshape(few * cf, lanes) for z in range(8)], axis=0
+                    [x_ref[x, z, y + k] for z in range(8) for x in range(4)], axis=0
                 )
                 for k in range(several)
             ],
@@ -198,7 +190,8 @@
                 for y in range(count // 2):
                     t = 4 * y + (2 if is_odd else 0)
                     word = encode(level[t] * scale) | (encode(level[t + 1] * scale) << 16)
-                    out_ref[woven(2 * k + q, y)] = word
+                    for x in range(4):
+                        out_ref[x, 2 * k + q, y] = word[2 * x : 2 * x + 2]
             return 0
 
         lax.fori_loop(0, own_ref.shape[1] // (2 * rows), step, 0)
@@ -257,7 +250,7 @@
     rows = voltages.reshape(cf, samp, channels).transpose(1, 0, 2)
     packed = call(pack_kernel, "pack", (peers, cf, LANES), jnp.bfloat16, [vmem], rows)
     turned = lax.all_to_all(packed, PEERS, split_axis=0, concat_axis=0, tiled=True)
-    turned = turned.reshape(peers // 4, 4, cf, LANES)
+    turned = turned.reshape(4, 8, y_count, cf, LANES)
     beams = feed_count * local
     own = call(
         beam_kernel,
@@ -275,7 +268,7 @@
     codes = call(
         tree_kernel,
         "tree",
-        (peers // 4, 8, LANES),
+        (4, 8, y_count, 2, LANES),
         jnp.int32,
         [smem, smem] + [vmem] * 4,
         place,
@@ -298,7 +291,7 @@
 
 def solution(mesh):
     devices = mesh.devices
-    fine = Mesh(devices.reshape((2, 2, 2, 4, 2, 2, 2, 2)), FEED + TIME)
+    fine = Mesh(devices.reshape((8, 4, 8, 2)), FEED + TIME)
     high, rest = dft_tables(8 * devices.shape[0])
     body = jax.shard_map(
         functools.partial(on_device),

time: 89.8 us -> 89.5 us (level)
  no operation moved by 1% of the time
where the time goes in v8:
time: 89.5 us; the launch traced here: 88.8 us
  blocking collectives  75.8 us (85%)
  Pallas kernels  5.59 us (6%)
  starting transfers between devices  4.38 us (5%)
  local copies, waits for them, and re-layouts  1.83 us (2%)
  waiting for transfers between devices  1.13 us (1%)
    all_to_all x1, blocking collectives, on_device(): lax.all_to_all(packed, PEERS, split_axis=0, concat_axis=0, tiled=True)  52.8 us
    all_to_all x1, blocking collectives, on_device(): back = lax.all_to_all(codes, PEERS, split_axis=0, concat_axis=0, tiled=True)  23 us
    pallas_call x4, Pallas kernels, call(): pl.pallas_call(kernel, in_specs=specs, out_specs=vmem, out_shape=jax.Shap...  5.59 us
    ppermute x1, starting transfers between devices, on_device(): other = lax.ppermute(own, 'core', [(0, 1), (1, 0)])  4.38 us
    unnamed x9, local copies, waits for them, and re-layouts  1.83 us
  transfers between devices with their start and end apart: 1, of which 1 were waited for; matrix products, arithmetic and copies ran while one was open for 0% of the time, Pallas kernels for 0%

profile of v8, /device:TPU:1, one launch (start us, length us, event | category | flops | bytes accessed | tf_op | source)
XLA Modules:
  0.0 88.8 jit_solution(15378469054759951580)
XLA Ops:
  0.0 1.8 %copy.8 = bf16[2,8,4,8192]{3,1,0,2:T(8,128)(2,1)S(1)} copy(bf16[2,8,4,8192]{3,2,1,0:T(4,128)(2,1)} %param.5) | data formatting | bytes 2097152 | tf_op args[0]
  1.8 0.8 pack.1
  2.7 0.0 copy-start
  2.7 0.0 copy-start.1
  2.7 52.8 %all_to_all.10 = bf16[256,16,128]{2,1,0:T(8,128)(2,1)S(1)} all-to-all(bf16[256,16,128]{2,1,0:T(8,128)(2,1)S(1)} %pack.1), channel_id=1, replica_groups=mesh['z'=8,'x'=4,'y'=8,'core'=2] {'x','z','y'}, dimensions={0} | all-to-all | bytes 2097152 | tf_op jit(solution)/shard_map/all_to_all | solution.py:252
  55.5 0.0 copy-done
  55.5 0.0 copy-done.1
  55.5 0.0 copy-start.2
  55.5 1.4 %beams.1.own_ref = bf16[16,64,128]{2,1,0:T(8,128)(2,1)S(1)} custom-call(bf16[512,512]{1,0:T(8,128)(2,1)S(1)} %copy-done.1, bf16[512,512]{1,0:T(8,128)(2,1)S(1)} %copy-done, bf16[4,8,8,16,128]{4,3,2,1,0:T(8,128)(2,1)S(1)} %bitcast.11), custom_call_target="tpu_custom_call" | custom-call | tf_op jit(solution)/shard_map/beams/pallas_call | solution.py:241
  57.0 0.0 copy-start.3
  57.0 4.4 %collective-permute-start = (bf16[16,64,128]{2,1,0:T(8,128)(2,1)S(1)}, bf16[16,64,128]{2,1,0:T(8,128)(2,1)S(1)}, u32[]{:S(2)}, u32[]{:S(2)}) collective-permute-start(bf16[16,64,128]{2,1,0:T(8,128)(2,1)S(1)} %beams.1.own_ref), channel_id=1, source_target_pairs={{0,1},{1,0},{2,3},{3,2},{4,5},{5,4},{6,7},{7,6},{8,9},{9,8},{10,11... | collective-permute-start | bytes 786440 | tf_op jit(solution)/shard_map/ppermute | solution.py:265
  61.4 1.1 %collective-permute-done.other_ref = bf16[16,64,128]{2,1,0:T(8,128)(2,1)S(1)} collective-permute-done((bf16[16,64,128]{2,1,0:T(8,128)(2,1)S(1)}, bf16[16,64,128]{2,1,0:T(8,128)(2,1)S(1)}, u32[]{:S(2)}, u32[]{:S(2)}) %collective-permute-start) | collective-permute-done | bytes 262176 | tf_op jit(solution)/shard_map/ppermute | solution.py:265
  62.5 0.0 copy-done.2
  62.5 0.0 copy-done.3
  62.5 1.9 %tree.1 = s32[4,8,8,2,128]{4,3,2,1,0:T(2,128)S(1)} custom-call(s32[1]{0:T(128)} %bitcast.place_ref, s32[1]{0:T(128)} %bitcast.1.core_ref, s32[64,128]{1,0:T(8,128)S(1)} %bitcast.15, s32[5,4096]{1,0:T(8,128)S(1)} %copy-done.2, bf16[16,64,128]{2,1,0:T(8,128)(2,1)S(1)} %beams.1.own_ref, bf16[16,64,128]{2,1,0:T(8,128)(2,1)S(1)} %collective-permute-done.other_ref), custom_call_target="tpu_custom_call" | custom-call | tf_op jit(solution)/shard_map/tree/pallas_call | solution.py:241
  64.4 23.0 %all_to_all.11 = s32[256,2,128]{2,1,0:T(2,128)S(1)} all-to-all(s32[256,2,128]{2,1,0:T(2,128)S(1)} %bitcast.13), channel_id=1, replica_groups=mesh['z'=8,'x'=4,'y'=8,'core'=2] {'x','z','y'}, dimensions={0} | all-to-all | bytes 524288 | tf_op jit(solution)/shard_map/all_to_all | solution.py:281
  87.3 1.4 %unpack.1 = f32[8,2,8192]{2,1,0:T(2,128)} custom-call(s32[64,8,128]{2,1,0:T(8,128)S(1)} %bitcast.14), custom_call_target="tpu_custom_call" | custom-call | tf_op jit(solution)/shard_map/unpack/pallas_call | solution.py:241
Async XLA Ops:
  2.7 52.9 %copy-start = (bf16[512,512]{1,0:T(8,128)(2,1)S(1)}, bf16[512,512]{1,0:T(8,128)(2,1)}, u32[]{:S(2)}) copy-start(bf16[512,512]{1,0:T(8,128)(2,1)} %constant.27.clone.rest_ref) | copy-start | bytes 1572868
  2.7 52.9 %copy-start.1 = (bf16[512,512]{1,0:T(8,128)(2,1)S(1)}, bf16[512,512]{1,0:T(8,128)(2,1)}, u32[]{:S(2)}) copy-start(bf16[512,512]{1,0:T(8,128)(2,1)} %constant.26.clone.high_ref) | copy-start | bytes 1572868
  55.5 7.0 %copy-start.2 = (s32[5,4096]{1,0:T(8,128)S(1)}, s32[5,4096]{1,0:T(8,128)}, u32[]{:S(2)}) copy-start(s32[5,4096]{1,0:T(8,128)} %off_ref.1) | copy-start | bytes 245764
  57.0 5.5 %copy-start.3 = (s32[8192]{0:T(1024)S(1)}, s32[8192]{0:T(1024)}, u32[]{:S(2)}) copy-start(s32[8192]{0:T(1024)} %param.6) | copy-start | bytes 98308
  57.0 5.5 %collective-permute-start = (bf16[16,64,128]{2,1,0:T(8,128)(2,1)S(1)}, bf16[16,64,128]{2,1,0:T(8,128)(2,1)S(1)}, u32[]{:S(2)}, u32[]{:S(2)}) collective-permute-start(bf16[16,64,128]{2,1,0:T(8,128)(2,1)S(1)} %beams.1.own_ref), channel_id=1, source_target_pairs={{0,1},{1,0},{2,3},{3,2},{4,5},{5,4},{6,7},{7,6},{8,9},{9,8},{10,11... | collective-permute-start | bytes 786440 | tf_op jit(solution)/shard_map/ppermute | solution.py:265

commit v9 on v6

--- a/solution.py
+++ b/solution.py
@@ -215,7 +215,7 @@
             out_ref[4 * k : 4 * k + 4, :, lanes] = value.reshape(4, 2, LANES)
         return 0
 
-    lax.fori_loop(0, tiles, step, 0, unroll=32)
+    lax.fori_loop(0, tiles, step, 0, unroll=64)
 
 
 def on_device(high, rest, voltages, channel_lag, offsets):

time: 88.8 us -> 88.6 us (level)
  no operation moved by 1% of the time
where the time goes in v9:
time: 88.6 us; the launch traced here: 87.8 us
  blocking collectives  74.4 us (84%)
  Pallas kernels  5.41 us (6%)
  starting transfers between devices  4.97 us (6%)
  local copies, waits for them, and re-layouts  1.82 us (2%)
  waiting for transfers between devices  1.13 us (1%)
    all_to_all x1, blocking collectives, on_device(): lax.all_to_all(packed, ('y', 'feed'), split_axis=0, concat_axis=0, tiled=...  51.5 us
    all_to_all x1, blocking collectives, on_device(): lax.all_to_all(codes, ('y', 'feed'), split_axis=0, concat_axis=0, tiled=T...  22.9 us
    pallas_call x4, Pallas kernels, call(): pl.pallas_call(kernel, in_specs=specs, out_specs=vmem, out_shape=jax.Shap...  5.41 us
    ppermute x1, starting transfers between devices, on_device(): other = lax.ppermute(own, 'core', [(0, 1), (1, 0)])  4.97 us
    unnamed x9, local copies, waits for them, and re-layouts  1.82 us
  transfers between devices with their start and end apart: 1, of which 1 were waited for; matrix products, arithmetic and copies ran while one was open for 0% of the time, Pallas kernels for 0%

profile of v9, /device:TPU:1, one launch (start us, length us, event | category | flops | bytes accessed | tf_op | source)
XLA Modules:
  0.0 87.8 jit_solution(2583916349109850846)
XLA Ops:
  0.0 1.8 %copy.8 = bf16[2,8,4,8192]{3,1,0,2:T(8,128)(2,1)S(1)} copy(bf16[2,8,4,8192]{3,2,1,0:T(4,128)(2,1)} %param.5) | data formatting | bytes 2097152 | tf_op args[0]
  1.8 0.8 pack.1
  2.7 0.0 copy-start
  2.7 0.0 copy-start.1
  2.7 51.5 %all_to_all.10 = bf16[256,16,128]{2,1,0:T(8,128)(2,1)S(1)} all-to-all(bf16[256,16,128]{2,1,0:T(8,128)(2,1)S(1)} %pack.1), channel_id=1, replica_groups=mesh['feed'=32,'y'=8,'core'=2] {'y','feed'}, dimensions={0} | all-to-all | bytes 2097152 | tf_op jit(solution)/shard_map/all_to_all | solution.py:243
  54.2 0.0 copy-done
  54.2 0.0 copy-done.1
  54.2 0.0 copy-start.2
  54.2 0.0 copy-start.3
  54.2 1.4 %beams.1.own_ref = bf16[16,64,128]{2,1,0:T(8,128)(2,1)S(1)} custom-call(bf16[512,512]{1,0:T(8,128)(2,1)S(1)} %copy-done.1, bf16[512,512]{1,0:T(8,128)(2,1)S(1)} %copy-done, bf16[8,32,16,128]{3,2,1,0:T(8,128)(2,1)S(1)} %bitcast.11), custom_call_target="tpu_custom_call" | custom-call | tf_op jit(solution)/shard_map/beams/pallas_call | solution.py:232
  55.6 5.0 %collective-permute-start = (bf16[16,64,128]{2,1,0:T(8,128)(2,1)S(1)}, bf16[16,64,128]{2,1,0:T(8,128)(2,1)S(1)}, u32[]{:S(2)}, u32[]{:S(2)}) collective-permute-start(bf16[16,64,128]{2,1,0:T(8,128)(2,1)S(1)} %beams.1.own_ref), channel_id=1, source_target_pairs={{0,1},{1,0},{2,3},{3,2},{4,5},{5,4},{6,7},{7,6},{8,9},{9,8},{10,11... | collective-permute-start | bytes 786440 | tf_op jit(solution)/shard_map/ppermute | solution.py:256
  60.6 1.1 %collective-permute-done.other_ref = bf16[16,64,128]{2,1,0:T(8,128)(2,1)S(1)} collective-permute-done((bf16[16,64,128]{2,1,0:T(8,128)(2,1)S(1)}, bf16[16,64,128]{2,1,0:T(8,128)(2,1)S(1)}, u32[]{:S(2)}, u32[]{:S(2)}) %collective-permute-start) | collective-permute-done | bytes 262176 | tf_op jit(solution)/shard_map/ppermute | solution.py:256
  61.7 0.0 copy-done.2
  61.7 0.0 copy-done.3
  61.7 1.9 %tree.1 = s32[8,8,8,128]{3,2,1,0:T(8,128)S(1)} custom-call(s32[1]{0:T(128)} %bitcast.place_ref, s32[1]{0:T(128)} %bitcast.1.core_ref, s32[64,128]{1,0:T(8,128)S(1)} %bitcast.15, s32[5,4096]{1,0:T(8,128)S(1)} %copy-done.2, bf16[16,64,128]{2,1,0:T(8,128)(2,1)S(1)} %beams.1.own_ref, bf16[16,64,128]{2,1,0:T(8,128)(2,1)S(1)} %collective-permute-done.other_ref), custom_call_target="tpu_custom_call" | custom-call | tf_op jit(solution)/shard_map/tree/pallas_call | solution.py:232
  63.6 22.9 %all_to_all.11 = s32[256,2,128]{2,1,0:T(2,128)S(1)} all-to-all(s32[256,2,128]{2,1,0:T(2,128)S(1)} %bitcast.13), channel_id=1, replica_groups=mesh['feed'=32,'y'=8,'core'=2] {'y','feed'}, dimensions={0} | all-to-all | bytes 524288 | tf_op jit(solution)/shard_map/all_to_all | solution.py:272
  86.6 1.3 %unpack.1 = f32[8,2,8192]{2,1,0:T(2,128)} custom-call(s32[64,8,128]{2,1,0:T(8,128)S(1)} %bitcast.14), custom_call_target="tpu_custom_call" | custom-call | tf_op jit(solution)/shard_map/unpack/pallas_call | solution.py:232
Async XLA Ops:
  2.7 51.5 %copy-start = (bf16[512,512]{1,0:T(8,128)(2,1)S(1)}, bf16[512,512]{1,0:T(8,128)(2,1)}, u32[]{:S(2)}) copy-start(bf16[512,512]{1,0:T(8,128)(2,1)} %constant.21.clone.rest_ref) | copy-start | bytes 1572868
  2.7 51.5 %copy-start.1 = (bf16[512,512]{1,0:T(8,128)(2,1)S(1)}, bf16[512,512]{1,0:T(8,128)(2,1)}, u32[]{:S(2)}) copy-start(bf16[512,512]{1,0:T(8,128)(2,1)} %constant.20.clone.high_ref) | copy-start | bytes 1572868
  54.2 7.6 %copy-start.2 = (s32[5,4096]{1,0:T(8,128)S(1)}, s32[5,4096]{1,0:T(8,128)}, u32[]{:S(2)}) copy-start(s32[5,4096]{1,0:T(8,128)} %off_ref.1) | copy-start | bytes 245764
  54.2 7.6 %copy-start.3 = (s32[8192]{0:T(1024)S(1)}, s32[8192]{0:T(1024)}, u32[]{:S(2)}) copy-start(s32[8192]{0:T(1024)} %param.6) | copy-start | bytes 98308
  55.6 6.1 %collective-permute-start = (bf16[16,64,128]{2,1,0:T(8,128)(2,1)S(1)}, bf16[16,64,128]{2,1,0:T(8,128)(2,1)S(1)}, u32[]{:S(2)}, u32[]{:S(2)}) collective-permute-start(bf16[16,64,128]{2,1,0:T(8,128)(2,1)S(1)} %beams.1.own_ref), channel_id=1, source_target_pairs={{0,1},{1,0},{2,3},{3,2},{4,5},{5,4},{6,7},{7,6},{8,9},{9,8},{10,11... | collective-permute-start | bytes 786440 | tf_op jit(solution)/shard_map/ppermute | solution.py:256
